TPU v7x, 32 devices: a whole 2x2x4 slice. The times are simulated.
32 devices in a mesh: grp: 1, res: 16 (over z, y, core), seq: 2 (over x).
Axes of the slice: x: 2, y: 2, z: 4, core: 2. Of those that a mesh axis runs over, the one named last changes fastest.
Arguments:
- alignment_activations: bfloat16 [16, 256, 64], P(('grp', 'seq'), 'res'), may hold values from -6 to 6
- alignment_row_mask: int32 [16], P(('grp', 'seq')), may hold values 0 or 1
- residue_mask: int32 [256], P('grp'), may hold values 0 or 1
- pair_head_logits: bfloat16 [8, 256, 256], P(None, ('grp', 'res')), may hold values from -300 to 300, as said below
- value_matrix: bfloat16 [64, 256], replicated, may hold values from -0.75 to 0.75
- gate_matrix: bfloat16 [64, 256], replicated, may hold values from -0.75 to 0.75
- output_matrix: bfloat16 [256, 64], replicated, may hold values from -0.375 to 0.375
- cotangent: bfloat16 [16, 256, 64], P(('grp', 'seq'), 'res'), may hold values from -6 to 6
Outputs:
- alignment_gradient: float32 [16, 256, 64], P(('grp', 'seq'), 'res')
- pair_logit_gradient: float32 [8, 256, 256], P(None, ('grp', 'res'), 'seq')
- value_weight_gradient: float32 [64, 256], P('grp')
- gate_weight_gradient: float32 [64, 256], P('grp')
- output_weight_gradient: float32 [256, 64], P('grp')
Inputs may be any that keep to these rules, and one draw needn't show every extreme that they name: `pair_head_logits`: bfloat16 logits.
All inputs are finite; a program needn't handle non-finite values. No bound on the sum of `alignment_row_mask` on one device may be relied on, other than what follows from the above.
Results may differ from a plain program's by a relative error of at most 0.0071.
Values may be sent and summed in bfloat16 or wider, within the bound.
No kernel may reach another device: no remote copies, remote signals or barrier semaphores. Data moves between devices by JAX's collectives and lax.ppermute only.
A program may use at most 64 MiB of HBM per device.

v0:
```python
import jax
import jax.numpy as jnp
from jax import lax
from jax.sharding import PartitionSpec as P


def layer_standardize(alignment_activations):
    activation_input = alignment_activations.astype(jnp.float32)
    mean_val = jnp.mean(activation_input, axis=-1, keepdims=True)
    centered = activation_input - mean_val
    variance = jnp.mean(centered * centered, axis=-1, keepdims=True)
    inverse_deviation = lax.rsqrt(variance + 1e-05)
    return (centered * inverse_deviation, inverse_deviation)


def gated_back(cot_rows, gate_act, row_keep, output_matrix):
    grad_mixed = lax.dot_general(
        cot_rows, output_matrix, (((2,), (1,)), ((), ())), preferred_element_type=jnp.float32
    )
    return (grad_mixed, (grad_mixed * gate_act * row_keep).astype(jnp.bfloat16))


def block_terms(
    weights, columns, values_all, gate_act, grad_mixed, grad_att, att_all, row_keep, head_count
):
    row_count, key_count, width = values_all.shape
    head_dim = width // head_count
    values_heads = values_all.reshape(row_count, key_count, head_count, head_dim)
    attended = jnp.einsum(
        "hij,sjhc->sihc", weights, values_heads, preferred_element_type=jnp.float32
    )
    attended = attended.reshape(row_count, -1, width)
    mixed_out = (gate_act * attended * row_keep).astype(jnp.bfloat16)
    gate_grad = (grad_mixed * attended * row_keep * gate_act * (1.0 - gate_act)).astype(
        jnp.bfloat16
    )
    att_heads = grad_att.reshape(row_count, -1, head_count, head_dim)
    pair_total = jnp.einsum(
        "sihc,sjhc->hij", att_heads, values_heads, preferred_element_type=jnp.float32
    )
    all_heads = att_all.reshape(row_count, key_count, head_count, head_dim)
    grad_values = jnp.einsum(
        "hij,sihc->sjhc", columns, all_heads, preferred_element_type=jnp.float32
    )
    grad_values = grad_values.reshape(row_count, -1, width).astype(jnp.bfloat16)
    return (pair_total, mixed_out, gate_grad, grad_values)


def local(
    alignment_activations,
    alignment_row_mask,
    residue_mask,
    pair_head_logits,
    value_matrix,
    gate_matrix,
    output_matrix,
    cotangent,
):
    head_count = pair_head_logits.shape[0]
    key_count = pair_head_logits.shape[2]
    unit_alignment, inverse_deviation = layer_standardize(alignment_activations)
    standardized_rows = unit_alignment.astype(jnp.bfloat16)
    key_live = residue_mask == 1
    scores = jnp.where(key_live[None, None, :], pair_head_logits.astype(jnp.float32), -10000.0)
    prob_full = jax.nn.softmax(scores, axis=-1)
    weights = prob_full.astype(jnp.bfloat16)
    columns = lax.all_to_all(weights, "res", split_axis=2, concat_axis=1, tiled=True)
    row_keep = alignment_row_mask.astype(jnp.float32)[:, None, None]
    gate_own = jax.nn.sigmoid(
        jnp.dot(standardized_rows, gate_matrix, preferred_element_type=jnp.float32)
    )
    mixed_own, att_own = gated_back(cotangent, gate_own, row_keep, output_matrix)
    normed_all, cot_all = (
        lax.all_gather(standardized_rows, "res", axis=1, tiled=True),
        lax.all_gather(cotangent, "res", axis=1, tiled=True),
    )
    values_all = jnp.dot(normed_all, value_matrix, preferred_element_type=jnp.float32).astype(
        jnp.bfloat16
    )
    gate_all = jax.nn.sigmoid(jnp.dot(normed_all, gate_matrix, preferred_element_type=jnp.float32))
    mixed_all, att_all = gated_back(cot_all, gate_all, row_keep, output_matrix)
    pair_total, mixed_out, gate_grad, grad_values = block_terms(
        weights, columns, values_all, gate_own, mixed_own, att_own, att_all, row_keep, head_count
    )
    output_weight_gradient = jnp.einsum(
        "sic,sid->cd", mixed_out, cotangent, preferred_element_type=jnp.float32
    )
    value_weight_gradient = jnp.einsum(
        "sic,sid->cd", standardized_rows, grad_values, preferred_element_type=jnp.float32
    )
    gate_weight_gradient = jnp.einsum(
        "sic,sid->cd", standardized_rows, gate_grad, preferred_element_type=jnp.float32
    )
    gradient_totals = lax.psum(
        (value_weight_gradient, gate_weight_gradient, output_weight_gradient), ("res", "seq")
    )
    gradient_standardized = jnp.dot(grad_values, value_matrix.T, preferred_element_type=jnp.float32)
    gradient_standardized = gradient_standardized + jnp.dot(
        gate_grad, gate_matrix.T, preferred_element_type=jnp.float32
    )
    leading_average = jnp.mean(gradient_standardized, axis=-1, keepdims=True)
    trailing_average = jnp.mean(gradient_standardized * unit_alignment, axis=-1, keepdims=True)
    alignment_gradient = inverse_deviation * (
        gradient_standardized - leading_average - unit_alignment * trailing_average
    )
    grad_prob = lax.psum(pair_total, "seq")
    full_grads = prob_full * (grad_prob - jnp.sum(prob_full * grad_prob, axis=-1, keepdims=True))
    share_width = key_count // lax.axis_size("seq")
    pair_logit_gradient = lax.dynamic_slice_in_dim(
        full_grads, lax.axis_index("seq") * share_width, share_width, 2
    )
    return (
        alignment_gradient,
        pair_logit_gradient,
        gradient_totals[0],
        gradient_totals[1],
        gradient_totals[2],
    )


def solution(mesh):
    return jax.shard_map(
        local,
        mesh=mesh,
        in_specs=(
            P(("grp", "seq"), "res", None),
            P(("grp", "seq")),
            P("grp"),
            P(None, ("grp", "res"), None),
            P(),
            P(),
            P(),
            P(("grp", "seq"), "res", None),
        ),
        out_specs=(
            P(("grp", "seq"), "res", None),
            P(None, ("grp", "res"), "seq"),
            P("grp", None),
            P("grp", None),
            P("grp", None),
        ),
        check_vma=False,
    )
```

profile of v0, /device:TPU:0, one launch (start us, length us, event | category | flops | bytes accessed | tf_op | source)
XLA Modules:
  0.0 212.0 jit_solution(8977656552240691935)
XLA Ops:
  7.2 0.8 convert_reduce_fusion
  8.1 0.9 fusion.20
  9.0 0.9 fusion.16
  9.9 24.6 %all_gather.7 = bf16[8,256,64]{2,1,0:T(8,128)(2,1)S(1)} all-gather(bf16[8,16,64]{2,1,0:T(8,128)(2,1)S(1)} %fusion.16), channel_id=1, replica_groups=mesh['grp'=1,'res'=16,'seq'=2] {'res'}, dimensions={1}, use_global_device_ids=true | all-gather | bytes 278528 | tf_op jit(solution)/shard_map/all_gather | solution.py:74
  34.5 0.7 convert_element_type.41
  35.1 0.9 fusion.6
  36.1 1.0 multiply_convert_fusion.2
  37.2 1.2 convolution_convert_fusion
  38.5 1.0 convolution_bitcast_fusion.1
  39.5 18.9 %all_gather.6 = bf16[8,256,64]{2,1,0:T(8,128)(2,1)S(1)} all-gather(bf16[8,16,64]{2,1,0:T(8,128)(2,1)S(1)} %copy-done.3), channel_id=1, replica_groups=mesh['grp'=1,'res'=16,'seq'=2] {'res'}, dimensions={1}, use_global_device_ids=true | all-gather | bytes 278528 | tf_op jit(solution)/shard_map/all_gather | solution.py:75
  58.4 0.5 fusion.34
  58.9 1.8 multiply_convert_fusion
  60.9 1.1 multiply_reduce_fusion
  62.0 0.3 copy.26
  62.3 0.8 convolution_bitcast_fusion
  63.1 1.2 reshape.63
  64.3 3.5 %all-to-all-start = ((bf16[16,2,1024]{2,1,0:T(2,128)(2,1)}), bf16[16,2,1024]{2,1,0:T(2,128)(2,1)S(1)}, u32[]{:S(2)}, u32[]{:S(2)}) async-start(bf16[16,2,1024]{2,1,0:T(2,128)(2,1)} %reshape.63), calls=%async_computation | async-start | bytes 131072 | tf_op jit(solution)/shard_map/all_to_all | solution.py:67
  67.9 0.3 copy.31
  68.5 0.8 convolution_bitcast_fusion.3
  69.3 0.7 dynamic-slice_multiply_fusion
  70.0 0.8 convolution_bitcast_fusion.2
  70.9 3.8 %all-to-all-done = bf16[16,2,1024]{2,1,0:T(2,128)(2,1)S(1)} async-done(((bf16[16,2,1024]{2,1,0:T(2,128)(2,1)}), bf16[16,2,1024]{2,1,0:T(2,128)(2,1)S(1)}, u32[]{:S(2)}, u32[]{:S(2)}) %all-to-all-start) | async-done | bytes 65568 | tf_op jit(solution)/shard_map/all_to_all | solution.py:67
  74.7 0.4 reshape.64
  75.1 0.3 copy.46
  75.5 0.5 reshape.55
  75.9 0.8 fusion.1
  77.2 0.8 convolution_bitcast_fusion.4
  78.4 0.8 fusion.19
  79.1 121.6 %all-reduce.6.cloned.1.call-done = (f32[64,256]{1,0:T(8,128)}, f32[64,256]{1,0:T(8,128)}, f32[256,64]{0,1:T(8,128)}) async-done(((f32[64,256]{1,0:T(8,128)}, f32[64,256]{1,0:T(8,128)}, f32[256,64]{0,1:T(8,128)}), (f32[64,256]{1,0:T(8,128)}, f32[64,256]{1,0:T(8,128)}, f32[256,64]{0,1:T(8,128)})) %all-reduce.6.cloned.1.call-update) | async-done | bytes 196624 | tf_op jit(solution)/shard_map/psum | solution.py:94
  200.7 1.5 copy.51
  202.2 1.5 copy.52
  203.7 1.5 copy.53
  (36 shorter events, 1.6 us)
Async XLA Ops:
  7.2 28.9 %copy-start = (bf16[256,64]{0,1:T(8,128)(2,1)S(1)}, bf16[256,64]{0,1:T(8,128)(2,1)}, u32[]{:S(2)}) copy-start(bf16[256,64]{0,1:T(8,128)(2,1)} %param.14) | copy-start | bytes 98308
  7.2 53.7 %all-reduce.4.cloned.1.call-start = ((), (), s32[]{:S(2)}) async-start(), calls=%async_computation.1 | async-start | bytes 262144 | tf_op jit(solution)/shard_map/psum | solution.py:106
  36.1 3.4 %copy-start.3 = (bf16[8,16,64]{2,1,0:T(8,128)(2,1)S(1)}, bf16[8,16,64]{2,1,0:T(8,128)(2,1)}, u32[]{:S(2)}) copy-start(bf16[8,16,64]{2,1,0:T(8,128)(2,1)} %param.15) | copy-start | bytes 49156
  38.5 20.4 %copy-start.5 = (bf16[64,256]{1,0:T(8,128)(2,1)S(1)}, bf16[64,256]{1,0:T(8,128)(2,1)}, u32[]{:S(2)}) copy-start(bf16[64,256]{1,0:T(8,128)(2,1)} %param.13) | copy-start | bytes 98308
  58.9 1.8 copy-start.7
  58.9 1.8 copy-start.6
  62.3 7.0 %copy-start.2 = (f32[8,16,256]{2,1,0:T(8,128)S(1)}, f32[8,16,256]{2,1,0:T(8,128)}, u32[]{:S(2)}) copy-start(f32[8,16,256]{2,1,0:T(8,128)} %all-reduce.4.cloned.1.call-done) | copy-start | bytes 393220
  64.3 10.4 %all-to-all-start = ((bf16[16,2,1024]{2,1,0:T(2,128)(2,1)}), bf16[16,2,1024]{2,1,0:T(2,128)(2,1)S(1)}, u32[]{:S(2)}, u32[]{:S(2)}) async-start(bf16[16,2,1024]{2,1,0:T(2,128)(2,1)} %reshape.63), calls=%async_computation | async-start | bytes 131072 | tf_op jit(solution)/shard_map/all_to_all | solution.py:67
  67.8 132.9 %all-reduce.6.cloned.1.call-start = ((), (), s32[]{:S(2)}) async-start(), calls=%async_computation.2 | async-start | bytes 393216 | tf_op jit(solution)/shard_map/psum | solution.py:94
  68.2 7.7 %copy-start.8 = (bf16[8,256,256]{1,2,0:T(8,128)(2,1)S(1)}, bf16[8,256,256]{1,2,0:T(8,128)(2,1)}, u32[]{:S(2)}) copy-start(bf16[8,256,256]{1,2,0:T(8,128)(2,1)} %multiply_convert_fusion) | copy-start | bytes 3145732
  75.1 2.0 copy-start.4
  75.1 3.0 %copy-start.1 = (bf16[8,16,64]{2,1,0:T(8,128)(2,1)S(1)}, bf16[8,16,64]{2,1,0:T(8,128)(2,1)}, u32[]{:S(2)}) copy-start(bf16[8,16,64]{2,1,0:T(8,128)(2,1)} %param.8) | copy-start | bytes 49156
Sparse Core Ops, SparseCore 0:
  39.6 18.7 all-reduce.3
  78.5 122.2 all-reduce.5
where the time goes:
time: 213 us; the launch traced here: 212 us
  waiting for transfers between devices  125 us (59%)
  blocking collectives  43.5 us (20%)
  between operations  14.3 us (7%)
  matrix products  10.8 us (5%)
  local copies, waits for them, and re-layouts  8.21 us (4%)
  other arithmetic  6.14 us (3%)
  starting transfers between devices  3.58 us (2%)
    psum x1, waiting for transfers between devices, local(): lax.psum((value_weight_gradient, gate_weight_gradient, output_weight_grad...  122 us
    all_gather x1, blocking collectives, local(): lax.all_gather(standardized_rows, 'res', axis=1, tiled=True)  24.6 us
    all_gather x1, blocking collectives, local(): lax.all_gather(cotangent, 'res', axis=1, tiled=True)  18.9 us
    unnamed x23, local copies, waits for them, and re-layouts  6.06 us
  transfers between devices with their start and end apart: 3, of which 2 were waited for; matrix products, arithmetic and copies ran while one was open for 3% of the time, Pallas kernels for 0%

commit v1 on v0

--- a/solution.py
+++ b/solution.py
@@ -1,7 +1,318 @@
+import functools
+
 import jax
 import jax.numpy as jnp
 from jax import lax
+from jax.experimental import pallas as pl
+from jax.experimental.pallas import tpu as pltpu
 from jax.sharding import PartitionSpec as P
+
+LANES = 128
+F32 = jnp.float32
+BF16 = jnp.bfloat16
+
+
+def dot(a, b):
+    return lax.dot_general(a, b, (((1,), (0,)), ((), ())), preferred_element_type=F32)
+
+
+def dot_nt(a, b):
+    return lax.dot_general(a, b, (((1,), (1,)), ((), ())), preferred_element_type=F32)
+
+
+def dot_tn(a, b):
+    return lax.dot_general(a, b, (((0,), (0,)), ((), ())), preferred_element_type=F32)
+
+
+def standardize(x):
+    x = x.astype(F32)
+    centered = x - jnp.mean(x, axis=-1, keepdims=True)
+    inv = lax.rsqrt(jnp.mean(centered * centered, axis=-1, keepdims=True) + 1e-05)
+    return centered * inv, inv
+
+
+def pack_kernel(acts_ref, cot_ref, logits_ref, live_ref, pack_ref, prob_ref):
+    rows, own, depth = acts_ref.shape
+    heads, _, keys = logits_ref.shape
+    unit, _ = standardize(acts_ref[...])
+    normed = unit.astype(BF16)
+    cot = cot_ref[...]
+    per = LANES // depth
+    blocks = rows // per
+    for b in range(blocks):
+        pack_ref[pl.ds(b * own, own), :] = jnp.concatenate(
+            [normed[b * per + k] for k in range(per)], axis=-1
+        )
+        pack_ref[pl.ds((blocks + b) * own, own), :] = jnp.concatenate(
+            [cot[b * per + k] for k in range(per)], axis=-1
+        )
+    live = live_ref[...] == 1
+    wide = keys // LANES
+    for h in range(heads):
+        scores = jnp.where(live, logits_ref[h].astype(F32), -10000.0)
+        e = jnp.exp(scores - jnp.max(scores, axis=-1, keepdims=True))
+        prob = e / jnp.sum(e, axis=-1, keepdims=True)
+        prob_ref[h] = prob
+        weights = prob.astype(BF16)
+        for w in range(wide):
+            pack_ref[pl.ds((2 * blocks + h * wide + w) * own, own), :] = weights[
+                :, w * LANES : (w + 1) * LANES
+            ]
+
+
+def main_kernel(
+    heads,
+    where_ref,
+    keep_ref,
+    acts_ref,
+    prob_ref,
+    all_ref,
+    value_ref,
+    gate_ref,
+    output_ref,
+    align_ref,
+    pair_own_ref,
+    pair_send_ref,
+    totals_ref,
+    att_ref,
+    val_grad_ref,
+    gate_grad_ref,
+):
+    rows, own, depth = acts_ref.shape
+    parts, _, _, _ = all_ref.shape
+    keys = parts * own
+    width = value_ref.shape[1]
+    dim = width // heads
+    quad = LANES // dim
+    groups = rows // quad
+    per = LANES // depth
+    blocks = rows // per
+    wide = keys // LANES
+    first = pl.multiple_of(where_ref[0] * own, own)
+    half = where_ref[1]
+
+    def lane_block(k):
+        return all_ref[:, k].reshape(keys, LANES)
+
+    span = quad // per
+    x = [
+        jnp.concatenate([lane_block(g * span + k) for k in range(span)], axis=1)
+        for g in range(groups)
+    ]
+    y = [
+        jnp.concatenate([lane_block(blocks + g * span + k) for k in range(span)], axis=1)
+        for g in range(groups)
+    ]
+    x_t = [a.T for a in x]
+    y_t = [a.T for a in y]
+
+    lane = lax.broadcasted_iota(jnp.int32, (1, LANES), 1)
+    slot = lane // dim
+    keep = []
+    for g in range(groups):
+        row = jnp.zeros((1, LANES), F32)
+        for k in range(quad):
+            row = jnp.where(slot == k, keep_ref[g * quad + k].astype(F32), row)
+        keep.append(row)
+    keep_row = jnp.concatenate(keep, axis=1)
+
+    src = lax.broadcasted_iota(jnp.int32, (width, 2 * LANES), 0)
+    dst = lax.broadcasted_iota(jnp.int32, (width, 2 * LANES), 1)
+    dst_slot = (dst % LANES) // dim
+    spread_to = (dst // LANES) * dim + dst % dim
+    mask_row = lax.broadcasted_iota(jnp.int32, (quad * depth, 2 * LANES), 0) // depth
+    mask_col = (lax.broadcasted_iota(jnp.int32, (quad * depth, 2 * LANES), 1) % LANES) // dim
+    diagonal = mask_row == mask_col
+    fold_slot = dst_slot[:depth]
+
+    def block_diagonal(ref, p):
+        spread = (src == spread_to + 2 * p * dim).astype(BF16)
+        wide_rows = dot(ref[...], spread)
+        tall = jnp.concatenate([wide_rows] * quad, axis=0)
+        return jnp.where(diagonal, tall, 0.0).astype(BF16)
+
+    def fold(total):
+        picked = total[:depth]
+        for k in range(1, quad):
+            picked = jnp.where(fold_slot == k, total[k * depth : (k + 1) * depth], picked)
+        out = []
+        for h in range(2):
+            part = picked[:, h * LANES : (h + 1) * LANES]
+            step = LANES // 2
+            while step >= dim:
+                part = part + pltpu.roll(part, step, 1)
+                step //= 2
+            out.append(part)
+        return out
+
+    folded = [[], [], []]
+    grad_normed = [jnp.zeros((own, quad * depth), F32) for _ in range(groups)]
+    sums = jnp.zeros((own, LANES), F32)
+    for p in range(heads // 2):
+        value_bd = block_diagonal(value_ref, p)
+        gate_bd = block_diagonal(gate_ref, p)
+        output_bd = block_diagonal(output_ref, p)
+        values = [dot(a, value_bd).astype(BF16) for a in x]
+        gates = [dot(a, gate_bd) for a in x]
+        mixes = [dot(a, output_bd) for a in y]
+        mixed_out, gate_grad, val_grad = [], [], []
+        for k in range(2):
+            h = 2 * p + k
+            cut = slice(k * LANES, (k + 1) * LANES)
+            weights = jnp.concatenate(
+                [lane_block(2 * blocks + h * wide + w) for w in range(wide)], axis=1
+            )
+            vals = jnp.concatenate([v[:, cut] for v in values], axis=1)
+            attended = dot(weights, vals)
+            gate = jax.nn.sigmoid(jnp.concatenate([v[:, cut] for v in gates], axis=1))
+            mixed = jnp.concatenate([v[:, cut] for v in mixes], axis=1)
+            kept = gate * keep_row
+            grad_att = mixed * kept
+            att_bf = grad_att.astype(BF16)
+            att_ref[h] = att_bf
+            mixed_out.append((kept * attended).astype(BF16))
+            gate_grad.append((grad_att * attended * (1.0 - gate)).astype(BF16))
+            val_grad.append(dot_tn(weights, att_bf).astype(BF16))
+            pair = dot_nt(att_ref[h, pl.ds(first, own), :], vals)
+            prob = prob_ref[h]
+            sums = jnp.where(lane == h, jnp.sum(prob * pair, axis=-1, keepdims=True), sums)
+            low, high = pair[:, : keys // 2], pair[:, keys // 2 :]
+            pair_own_ref[h] = jnp.where(half == 0, low, high)
+            pair_send_ref[h] = jnp.where(half == 0, high, low)
+        totals = [None, None, None]
+        for g in range(groups):
+            cut = slice(g * LANES, (g + 1) * LANES)
+            mo = jnp.concatenate([a[:, cut] for a in mixed_out], axis=1)
+            gg = jnp.concatenate([a[:, cut] for a in gate_grad], axis=1)
+            vg = jnp.concatenate([a[:, cut] for a in val_grad], axis=1)
+            gate_grad_ref[p * groups + g] = gg
+            val_grad_ref[p * groups + g] = vg
+            grad_normed[g] = (
+                grad_normed[g]
+                + dot_nt(val_grad_ref[p * groups + g, pl.ds(first, own), :], value_bd)
+                + dot_nt(gate_grad_ref[p * groups + g, pl.ds(first, own), :], gate_bd)
+            )
+            for t, (left, right) in enumerate(((x_t, vg), (x_t, gg), (y_t, mo))):
+                term = dot(left[g], right)
+                totals[t] = term if totals[t] is None else totals[t] + term
+        for t in range(3):
+            folded[t].extend(fold(totals[t]))
+
+    pair_send_ref[heads] = sums
+    pair_own_ref[heads] = sums
+    for t in range(3):
+        cols = []
+        for b in range(width // LANES):
+            block = folded[t][b * quad]
+            for k in range(1, quad):
+                block = jnp.where(slot == k, folded[t][b * quad + k], block)
+            cols.append(block)
+        totals_ref[pl.ds(t * depth, depth), :] = jnp.concatenate(cols, axis=1).astype(BF16)
+
+    unit, inv = standardize(acts_ref[...])
+    for s in range(rows):
+        g, k = divmod(s, quad)
+        grad = grad_normed[g][:, k * depth : (k + 1) * depth]
+        lead = jnp.mean(grad, axis=-1, keepdims=True)
+        trail = jnp.mean(grad * unit[s], axis=-1, keepdims=True)
+        align_ref[s] = inv[s] * (grad - lead - unit[s] * trail)
+
+
+def last_kernel(
+    where_ref, prob_ref, own_ref, got_ref, totals_ref, more_ref, pair_ref, value_ref, gate_ref, output_ref
+):
+    heads = prob_ref.shape[0]
+    share = own_ref.shape[2]
+    half = where_ref[1]
+    sums = own_ref[heads] + got_ref[heads]
+    for h in range(heads):
+        prob = jnp.where(half == 0, prob_ref[h, :, :share], prob_ref[h, :, share:])
+        pair_ref[h] = prob * (own_ref[h] + got_ref[h] - sums[:, h : h + 1])
+    depth = value_ref.shape[0]
+    for t, ref in enumerate((value_ref, gate_ref, output_ref)):
+        rows = pl.ds(t * depth, depth)
+        ref[...] = totals_ref[rows, :].astype(F32) + more_ref[rows, :].astype(F32)
+
+
+def call(kernel, outs, spaces, scratch=()):
+    spec = {
+        "v": pl.BlockSpec(memory_space=pltpu.VMEM),
+        "s": pl.BlockSpec(memory_space=pltpu.SMEM),
+    }
+    return pl.pallas_call(
+        kernel,
+        out_shape=[jax.ShapeDtypeStruct(s, d) for s, d in outs],
+        in_specs=[spec[c] for c in spaces],
+        out_specs=[spec["v"]] * len(outs),
+        scratch_shapes=list(scratch),
+        compiler_params=pltpu.CompilerParams(vmem_limit_bytes=48 * 1024 * 1024),
+    )
+
+
+def local_gathered(
+    alignment_activations,
+    alignment_row_mask,
+    residue_mask,
+    pair_head_logits,
+    value_matrix,
+    gate_matrix,
+    output_matrix,
+    cotangent,
+):
+    rows, own, depth = alignment_activations.shape
+    heads, _, keys = pair_head_logits.shape
+    width = value_matrix.shape[1]
+    parts = keys // own
+    lanes = (2 * rows * depth + heads * keys) // LANES
+    where = jnp.stack([lax.axis_index("res"), lax.axis_index("seq")]).astype(jnp.int32)
+    packed, prob = call(
+        pack_kernel, [((lanes * own, LANES), BF16), ((heads, own, keys), F32)], "vvvv"
+    )(alignment_activations, cotangent, pair_head_logits, residue_mask.reshape(1, keys))
+    gathered = lax.all_gather(packed, "res", axis=0, tiled=True)
+    gathered = gathered.reshape(parts, lanes, own, LANES)
+    share = keys // 2
+    align, pair_own, pair_send, totals = call(
+        functools.partial(main_kernel, heads),
+        [
+            ((rows, own, depth), F32),
+            ((heads + 1, own, share), F32),
+            ((heads + 1, own, share), F32),
+            ((3 * depth, width), BF16),
+        ],
+        "ssvvvvvv",
+        [pltpu.VMEM((heads, keys, 2 * LANES), BF16)] * 3,
+    )(
+        where,
+        alignment_row_mask,
+        alignment_activations,
+        prob,
+        gathered,
+        value_matrix,
+        gate_matrix,
+        output_matrix.T,
+    )
+    swap = [(0, 1), (1, 0)]
+    pair_got = lax.ppermute(pair_send, "seq", swap)
+    totals_got = lax.ppermute(totals, "seq", swap)
+    pair, value_total, gate_total, output_total = call(
+        last_kernel,
+        [((heads, own, share), F32)] + [((depth, width), F32)] * 3,
+        "svvvvv",
+    )(where, prob, pair_own, pair_got, totals, totals_got)
+    return align, pair, value_total, gate_total, output_total.T
+
+
+def fits(mesh, rows, own, depth, heads, keys, width):
+    dim = width // heads
+    return (
+        mesh.shape["seq"] == 2
+        and keys == 2 * LANES
+        and own % 16 == 0
+        and depth == 2 * dim
+        and dim == LANES // 4
+        and heads % 4 == 0
+        and rows == 8
+    )
 
 
 def layer_standardize(alignment_activations):
@@ -118,9 +429,18 @@
     )
 
 
+def pick(mesh, *arrays):
+    rows, own, depth = arrays[0].shape
+    heads, _, keys = arrays[3].shape
+    width = arrays[4].shape[1]
+    if fits(mesh, rows, own, depth, heads, keys, width):
+        return local_gathered(*arrays)
+    return local(*arrays)
+
+
 def solution(mesh):
     return jax.shard_map(
-        local,
+        functools.partial(pick, mesh),
         mesh=mesh,
         in_specs=(
             P(("grp", "seq"), "res", None),

time: 213 us -> 80.1 us (0.38)
  waiting for transfers between devices: 125 us -> 47 us
  blocking collectives: 43.5 us -> 0 us
  matrix products: 10.8 us -> 0 us
  Pallas kernels: 0 us -> 8.2 us
  other arithmetic: 6.14 us -> 0.08 us
    psum x2 -> x0, waiting for transfers between devices: 122 us -> none  [the longest x1 122 us: local(): lax.psum((value_weight_gradient, gate_weight_gradient, output_weight_grad...]
    all_gather x2 -> x0, blocking collectives: 43.5 us -> none  [the longest x1 24.6 us: local(): lax.all_gather(standardized_rows, 'res', axis=1, tiled=True)]
    all_gather x0 -> x1, waiting for transfers between devices: none -> 42.4 us  [local_gathered(): gathered = lax.all_gather(packed, 'res', axis=0, tiled=True)]
    dot_general x13 -> x0, matrix products: 10.8 us -> none  [the longest x1 1.78 us: local(): jnp.dot(normed_all, gate_matrix, preferred_element_type=jnp.float32)]
    pallas_call x0 -> x3, Pallas kernels: none -> 8.2 us  [the longest x1 6.03 us: local_gathered(): call(functools.partial(main_kernel, heads), [((rows, own, depth), F32), (...]
    ppermute x0 -> x2, waiting for transfers between devices: none -> 4.52 us  [the longest x1 4.52 us: local_gathered(): pair_got = lax.ppermute(pair_send, 'seq', swap)]
    all_to_all x1 -> x0, waiting for transfers between devices: 3.83 us -> none  [local(): lax.all_to_all(weights, 'res', split_axis=2, concat_axis=1, tiled=True)]
    all_to_all x1 -> x0, starting transfers between devices: 3.5 us -> none  [local(): lax.all_to_all(weights, 'res', split_axis=2, concat_axis=1, tiled=True)]
  transfers between devices with their start and end apart: 3 -> 3, of which waited for: 2 -> 2; matrix products, arithmetic and copies ran while one was open for 3% -> 0% of each run, Pallas kernels for 0% -> 0%
where the time goes in v1:
time: 80.1 us; the launch traced here: 79.5 us
  waiting for transfers between devices  47 us (59%)
  between operations  14.1 us (18%)
  Pallas kernels  8.2 us (10%)
  local copies, waits for them, and re-layouts  8.12 us (10%)
  starting transfers between devices  2.06 us (3%)
    all_gather x1, waiting for transfers between devices, local_gathered(): gathered = lax.all_gather(packed, 'res', axis=0, tiled=True)  42.4 us
    unnamed x20, local copies, waits for them, and re-layouts  8.12 us
    pallas_call x1, Pallas kernels, local_gathered(): call(functools.partial(main_kernel, heads), [((rows, own, depth), F32), (...  6.03 us
    ppermute x1, waiting for transfers between devices, local_gathered(): pair_got = lax.ppermute(pair_send, 'seq', swap)  4.52 us
  transfers between devices with their start and end apart: 3, of which 2 were waited for; matrix products, arithmetic and copies ran while one was open for 0% of the time, Pallas kernels for 0%

profile of v1, /device:TPU:0, one launch (start us, length us, event | category | flops | bytes accessed | tf_op | source)
XLA Modules:
  0.0 79.5 jit_solution(11358970023509309864)
XLA Ops:
  7.2 0.0 all-gather.2.cloned.1.call-start
  7.2 0.0 copy-start.1
  7.2 0.7 copy-done.1
  8.0 0.0 copy-start.3
  8.0 0.8 %copy-done.3 = bf16[8,16,256]{2,1,0:T(8,128)(2,1)S(1)} copy-done((bf16[8,16,256]{2,1,0:T(8,128)(2,1)S(1)}, bf16[8,16,256]{2,1,0:T(8,128)(2,1)}, u32[]{:S(2)}) %copy-start.3) | copy-done | bytes 65560
  8.8 0.0 copy-start.7
  8.8 0.8 copy-done.7
  9.6 0.0 copy-start.8
  9.6 0.7 copy-done.8
  10.3 0.9 %shard_map.119 = (bf16[384,128]{1,0:T(8,128)(2,1)}, f32[8,16,256]{2,1,0:T(8,128)S(1)}) custom-call(bf16[8,16,64]{2,1,0:T(8,128)(2,1)S(1)} %copy-done.1, bf16[8,16,64]{2,1,0:T(8,128)(2,1)S(1)} %copy-done.7, bf16[8,16,256]{2,1,0:T(8,128)(2,1)S(1)} %copy-done.3, s32[1,256]{1,0:T(1,128)S(1)} %bitcast.8), custom_call_target="tpu_custom_call" | custom-call | tf_op jit(solution)/shard_map/pallas_call | solution.py:268
  11.2 0.0 all-gather.2.cloned.1.call-update
  11.2 0.1 pad_add_fusion.where_ref
  11.3 42.4 %all-gather.2.cloned.1.call-done = bf16[6144,128]{1,0:T(8,128)(2,1)} async-done(((bf16[384,128]{1,0:T(8,128)(2,1)}), bf16[6144,128]{1,0:T(8,128)(2,1)}) %all-gather.2.cloned.1.call-update) | async-done | bytes 1572880 | tf_op jit(solution)/shard_map/all_gather | solution.py:271
  53.7 0.0 copy-start
  53.7 1.4 %copy-done = bf16[6144,128]{1,0:T(8,128)(2,1)S(1)} copy-done((bf16[6144,128]{1,0:T(8,128)(2,1)S(1)}, bf16[6144,128]{1,0:T(8,128)(2,1)}, u32[]{:S(2)}) %copy-start) | copy-done | bytes 1572888
  55.1 0.0 copy-start.2
  55.1 0.8 copy-done.2
  55.9 0.0 copy-start.4
  55.9 0.8 copy-done.4
  56.6 0.0 copy-start.5
  56.6 0.8 copy-done.5
  57.4 0.0 copy-start.6
  57.4 0.8 copy-done.6
  58.1 0.0 copy-start.9
  58.1 0.7 copy-done.9
  58.8 6.0 %shard_map.120 = (f32[8,16,64]{2,1,0:T(8,128)}, f32[9,16,128]{2,1,0:T(8,128)S(1)}, f32[9,16,128]{2,1,0:T(8,128)S(1)}, bf16[192,256]{1,0:T(8,128)(2,1)S(1)}) custom-call(s32[2]{0:T(128)S(1)} %pad_add_fusion.where_ref, s32[8]{0:T(128)S(1)} %copy-done.9, bf16[8,16,64]{2,1,0:T(8,128)(2,1)S(1)} %copy-done.2, f32[8,16,256]{2,1,0:T(8,128)S(1)} %get-tuple-element.15.prob_ref, ...), custom_call_target="tpu_custom_call" | custom-call | tf_op jit(solution)/shard_map/pallas_call | solution.py:274
  64.8 1.5 %collective-permute-start.1 = (bf16[192,256]{1,0:T(8,128)(2,1)S(1)}, bf16[192,256]{1,0:T(8,128)(2,1)S(1)}, u32[]{:S(2)}, u32[]{:S(2)}) collective-permute-start(bf16[192,256]{1,0:T(8,128)(2,1)S(1)} %get-tuple-element.20.totals_ref), channel_id=1, source_target_pairs={{0,1},{1,0},{2,3},{3,2},{4,5},{5,4},{6,7},{7,6},{8,9},{9,8},{10,11... | collective-permute-start | bytes 294920 | tf_op jit(solution)/shard_map/ppermute | solution.py:296
  66.3 0.6 collective-permute-start
  66.9 4.5 %collective-permute-done.got_ref = f32[9,16,128]{2,1,0:T(8,128)S(1)} collective-permute-done((f32[9,16,128]{2,1,0:T(8,128)S(1)}, f32[9,16,128]{2,1,0:T(8,128)S(1)}, u32[]{:S(2)}, u32[]{:S(2)}) %collective-permute-start) | collective-permute-done | bytes 73760 | tf_op jit(solution)/shard_map/ppermute | solution.py:295
  71.4 0.0 collective-permute-done.1.more_ref
  71.4 1.3 %shard_map.121 = (f32[8,16,128]{2,1,0:T(8,128)}, f32[64,256]{1,0:T(8,128)}, f32[64,256]{1,0:T(8,128)}, f32[64,256]{1,0:T(8,128)}) custom-call(s32[2]{0:T(128)S(1)} %pad_add_fusion.where_ref, f32[8,16,256]{2,1,0:T(8,128)S(1)} %get-tuple-element.15.prob_ref, f32[9,16,128]{2,1,0:T(8,128)S(1)} %get-tuple-element.18.own_ref, ...), custom_call_target="tpu_custom_call" | custom-call | tf_op jit(solution)/shard_map/pallas_call | solution.py:297
Async XLA Ops:
  7.2 46.5 %all-gather.2.cloned.1.call-start = ((), (), s32[]{:S(2)}) async-start(), calls=%async_computation | async-start | bytes 1671168 | tf_op jit(solution)/shard_map/all_gather | solution.py:271
  7.2 0.8 copy-start.1
  8.0 0.8 %copy-start.3 = (bf16[8,16,256]{2,1,0:T(8,128)(2,1)S(1)}, bf16[8,16,256]{2,1,0:T(8,128)(2,1)}, u32[]{:S(2)}) copy-start(bf16[8,16,256]{2,1,0:T(8,128)(2,1)} %logits_ref.1) | copy-start | bytes 196612
  8.8 0.8 copy-start.7
  9.6 0.7 copy-start.8
  53.7 1.4 %copy-start = (bf16[6144,128]{1,0:T(8,128)(2,1)S(1)}, bf16[6144,128]{1,0:T(8,128)(2,1)}, u32[]{:S(2)}) copy-start(bf16[6144,128]{1,0:T(8,128)(2,1)} %all-gather.2.cloned.1.call-done) | copy-start | bytes 4718596
  55.1 0.8 copy-start.2
  55.9 0.8 copy-start.4
  56.6 0.8 copy-start.5
  57.4 0.8 copy-start.6
  58.1 0.7 copy-start.9
  64.8 6.5 %collective-permute-start.1 = (bf16[192,256]{1,0:T(8,128)(2,1)S(1)}, bf16[192,256]{1,0:T(8,128)(2,1)S(1)}, u32[]{:S(2)}, u32[]{:S(2)}) collective-permute-start(bf16[192,256]{1,0:T(8,128)(2,1)S(1)} %get-tuple-element.20.totals_ref), channel_id=1, source_target_pairs={{0,1},{1,0},{2,3},{3,2},{4,5},{5,4},{6,7},{7,6},{8,9},{9,8},{10,11... | collective-permute-start | bytes 294920 | tf_op jit(solution)/shard_map/ppermute | solution.py:296
  66.3 5.1 %collective-permute-start = (f32[9,16,128]{2,1,0:T(8,128)S(1)}, f32[9,16,128]{2,1,0:T(8,128)S(1)}, u32[]{:S(2)}, u32[]{:S(2)}) collective-permute-start(f32[9,16,128]{2,1,0:T(8,128)S(1)} %get-tuple-element.19), channel_id=1, source_target_pairs={{0,1},{1,0},{2,3},{3,2},{4,5},{5,4},{6,7},{7,6},{8,9},{9,8},{10,11... | collective-permute-start | bytes 221192 | tf_op jit(solution)/shard_map/ppermute | solution.py:295
Sparse Core Ops, SparseCore 0:
  11.3 42.3 all-gather.1

commit v2 on v1

--- a/solution.py
+++ b/solution.py
@@ -31,23 +31,44 @@
     return centered * inv, inv
 
 
-def pack_kernel(acts_ref, cot_ref, logits_ref, live_ref, pack_ref, prob_ref):
+def fetch(sources, targets, sems):
+    copies = [
+        pltpu.make_async_copy(src, dst, sems.at[i])
+        for i, (src, dst) in enumerate(zip(sources, targets))
+    ]
+    for copy in copies:
+        copy.start()
+    return copies
+
+
+def pack_kernel(
+    acts_hbm, cot_hbm, logits_hbm, live_hbm, pack_ref, prob_ref,
+    acts_ref, cot_ref, logits_ref, live_ref, sems,
+):
+    copies = fetch(
+        (acts_hbm, cot_hbm, logits_hbm, live_hbm), (acts_ref, cot_ref, logits_ref, live_ref), sems
+    )
     rows, own, depth = acts_ref.shape
     heads, _, keys = logits_ref.shape
+    per = LANES // depth
+    blocks = rows // per
+    wide = keys // LANES
+    copies[0].wait()
     unit, _ = standardize(acts_ref[...])
     normed = unit.astype(BF16)
-    cot = cot_ref[...]
-    per = LANES // depth
-    blocks = rows // per
     for b in range(blocks):
         pack_ref[pl.ds(b * own, own), :] = jnp.concatenate(
             [normed[b * per + k] for k in range(per)], axis=-1
         )
+    copies[1].wait()
+    cot = cot_ref[...]
+    for b in range(blocks):
         pack_ref[pl.ds((blocks + b) * own, own), :] = jnp.concatenate(
             [cot[b * per + k] for k in range(per)], axis=-1
         )
+    copies[2].wait()
+    copies[3].wait()
     live = live_ref[...] == 1
-    wide = keys // LANES
     for h in range(heads):
         scores = jnp.where(live, logits_ref[h].astype(F32), -10000.0)
         e = jnp.exp(scores - jnp.max(scores, axis=-1, keepdims=True))
@@ -60,29 +81,68 @@
             ]
 
 
+def prepare_kernel(
+    heads,
+    keep_ref,
+    acts_ref,
+    value_ref,
+    gate_ref,
+    output_ref,
+    spread_ref,
+    keep_row_ref,
+    unit_ref,
+    inv_ref,
+):
+    rows, _, depth = acts_ref.shape
+    width = value_ref.shape[1]
+    dim = width // heads
+    quad = LANES // dim
+    slot = lax.broadcasted_iota(jnp.int32, (1, LANES), 1) // dim
+    for g in range(rows // quad):
+        row = jnp.zeros((1, LANES), F32)
+        for k in range(quad):
+            row = jnp.where(slot == k, keep_ref[g * quad + k].astype(F32), row)
+        keep_row_ref[:, g * LANES : (g + 1) * LANES] = row
+    src = lax.broadcasted_iota(jnp.int32, (width, 2 * LANES), 0)
+    dst = lax.broadcasted_iota(jnp.int32, (width, 2 * LANES), 1)
+    spread_to = (dst // LANES) * dim + dst % dim
+    mask_row = lax.broadcasted_iota(jnp.int32, (quad * depth, 2 * LANES), 0) // depth
+    mask_col = (lax.broadcasted_iota(jnp.int32, (quad * depth, 2 * LANES), 1) % LANES) // dim
+    diagonal = mask_row == mask_col
+    for p in range(heads // 2):
+        spread = (src == spread_to + 2 * p * dim).astype(BF16)
+        for t, ref in enumerate((value_ref, gate_ref, output_ref)):
+            tall = jnp.concatenate([dot(ref[...], spread)] * quad, axis=0)
+            spread_ref[t, p] = jnp.where(diagonal, tall, 0.0).astype(BF16)
+    unit, inv = standardize(acts_ref[...])
+    unit_ref[...] = unit
+    inv_ref[...] = jnp.broadcast_to(inv, unit.shape)
+
+
 def main_kernel(
     heads,
     where_ref,
-    keep_ref,
-    acts_ref,
     prob_ref,
-    all_ref,
-    value_ref,
-    gate_ref,
-    output_ref,
+    near_ref,
+    far_ref,
+    spread_ref,
+    keep_row_ref,
+    unit_ref,
+    inv_ref,
     align_ref,
     pair_own_ref,
     pair_send_ref,
     totals_ref,
+    all_ref,
     att_ref,
     val_grad_ref,
     gate_grad_ref,
 ):
-    rows, own, depth = acts_ref.shape
+    rows, own, depth = unit_ref.shape
     parts, _, _, _ = all_ref.shape
     keys = parts * own
-    width = value_ref.shape[1]
-    dim = width // heads
+    dim = keep_row_ref.shape[1] // rows
+    width = heads * dim
     quad = LANES // dim
     groups = rows // quad
     per = LANES // depth
@@ -90,6 +150,10 @@
     wide = keys // LANES
     first = pl.multiple_of(where_ref[0] * own, own)
     half = where_ref[1]
+    for r in range(parts):
+        away = where_ref[0] ^ r
+        spot = (away // 2 % 2) * (parts // 4) + away // 4
+        all_ref[r] = jnp.where(away % 2 == 0, near_ref[spot], far_ref[spot])
 
     def lane_block(k):
         return all_ref[:, k].reshape(keys, LANES)
@@ -108,28 +172,8 @@
 
     lane = lax.broadcasted_iota(jnp.int32, (1, LANES), 1)
     slot = lane // dim
-    keep = []
-    for g in range(groups):
-        row = jnp.zeros((1, LANES), F32)
-        for k in range(quad):
-            row = jnp.where(slot == k, keep_ref[g * quad + k].astype(F32), row)
-        keep.append(row)
-    keep_row = jnp.concatenate(keep, axis=1)
-
-    src = lax.broadcasted_iota(jnp.int32, (width, 2 * LANES), 0)
-    dst = lax.broadcasted_iota(jnp.int32, (width, 2 * LANES), 1)
-    dst_slot = (dst % LANES) // dim
-    spread_to = (dst // LANES) * dim + dst % dim
-    mask_row = lax.broadcasted_iota(jnp.int32, (quad * depth, 2 * LANES), 0) // depth
-    mask_col = (lax.broadcasted_iota(jnp.int32, (quad * depth, 2 * LANES), 1) % LANES) // dim
-    diagonal = mask_row == mask_col
-    fold_slot = dst_slot[:depth]
-
-    def block_diagonal(ref, p):
-        spread = (src == spread_to + 2 * p * dim).astype(BF16)
-        wide_rows = dot(ref[...], spread)
-        tall = jnp.concatenate([wide_rows] * quad, axis=0)
-        return jnp.where(diagonal, tall, 0.0).astype(BF16)
+    keep_row = keep_row_ref[...]
+    fold_slot = (lax.broadcasted_iota(jnp.int32, (depth, 2 * LANES), 1) % LANES) // dim
 
     def fold(total):
         picked = total[:depth]
@@ -149,9 +193,9 @@
     grad_normed = [jnp.zeros((own, quad * depth), F32) for _ in range(groups)]
     sums = jnp.zeros((own, LANES), F32)
     for p in range(heads // 2):
-        value_bd = block_diagonal(value_ref, p)
-        gate_bd = block_diagonal(gate_ref, p)
-        output_bd = block_diagonal(output_ref, p)
+        value_bd = spread_ref[0, p]
+        gate_bd = spread_ref[1, p]
+        output_bd = spread_ref[2, p]
         values = [dot(a, value_bd).astype(BF16) for a in x]
         gates = [dot(a, gate_bd) for a in x]
         mixes = [dot(a, output_bd) for a in y]
@@ -209,13 +253,12 @@
             cols.append(block)
         totals_ref[pl.ds(t * depth, depth), :] = jnp.concatenate(cols, axis=1).astype(BF16)
 
-    unit, inv = standardize(acts_ref[...])
     for s in range(rows):
         g, k = divmod(s, quad)
         grad = grad_normed[g][:, k * depth : (k + 1) * depth]
         lead = jnp.mean(grad, axis=-1, keepdims=True)
-        trail = jnp.mean(grad * unit[s], axis=-1, keepdims=True)
-        align_ref[s] = inv[s] * (grad - lead - unit[s] * trail)
+        trail = jnp.mean(grad * unit_ref[s], axis=-1, keepdims=True)
+        align_ref[s] = inv_ref[s] * (grad - lead - unit_ref[s] * trail)
 
 
 def last_kernel(
@@ -238,6 +281,7 @@
     spec = {
         "v": pl.BlockSpec(memory_space=pltpu.VMEM),
         "s": pl.BlockSpec(memory_space=pltpu.SMEM),
+        "h": pl.BlockSpec(memory_space=pltpu.HBM),
     }
     return pl.pallas_call(
         kernel,
@@ -266,10 +310,35 @@
     lanes = (2 * rows * depth + heads * keys) // LANES
     where = jnp.stack([lax.axis_index("res"), lax.axis_index("seq")]).astype(jnp.int32)
     packed, prob = call(
-        pack_kernel, [((lanes * own, LANES), BF16), ((heads, own, keys), F32)], "vvvv"
+        pack_kernel,
+        [((lanes * own, LANES), BF16), ((heads, own, keys), F32)],
+        "hhhh",
+        [
+            pltpu.VMEM((rows, own, depth), BF16),
+            pltpu.VMEM((rows, own, depth), BF16),
+            pltpu.VMEM((heads, own, keys), BF16),
+            pltpu.VMEM((1, keys), jnp.int32),
+            pltpu.SemaphoreType.DMA((4,)),
+        ],
     )(alignment_activations, cotangent, pair_head_logits, residue_mask.reshape(1, keys))
-    gathered = lax.all_gather(packed, "res", axis=0, tiled=True)
-    gathered = gathered.reshape(parts, lanes, own, LANES)
+
+    def swapped(array, bits):
+        return lax.ppermute(array, "res", [(i, i ^ bits) for i in range(parts)])
+
+    spread, keep_row, unit, inv = call(
+        functools.partial(prepare_kernel, heads),
+        [
+            ((3, heads // 2, 2 * LANES, 2 * LANES), BF16),
+            ((1, rows * width // heads), F32),
+            ((rows, own, depth), F32),
+            ((rows, own, depth), F32),
+        ],
+        "svvvv",
+    )(alignment_row_mask, alignment_activations, value_matrix, gate_matrix, output_matrix.T)
+    line = jnp.concatenate([packed] + [swapped(packed, 4 * k) for k in range(1, parts // 4)])
+    plane = jnp.concatenate([line, swapped(line, 2)])
+    other = swapped(plane, 1)
+    near, far = (a.reshape(parts // 2, lanes, own, LANES) for a in (plane, other))
     share = keys // 2
     align, pair_own, pair_send, totals = call(
         functools.partial(main_kernel, heads),
@@ -279,18 +348,10 @@
             ((heads + 1, own, share), F32),
             ((3 * depth, width), BF16),
         ],
-        "ssvvvvvv",
-        [pltpu.VMEM((heads, keys, 2 * LANES), BF16)] * 3,
-    )(
-        where,
-        alignment_row_mask,
-        alignment_activations,
-        prob,
-        gathered,
-        value_matrix,
-        gate_matrix,
-        output_matrix.T,
-    )
+        "svvvvvvv",
+        [pltpu.VMEM((parts, lanes, own, LANES), BF16)]
+        + [pltpu.VMEM((heads, keys, 2 * LANES), BF16)] * 3,
+    )(where, prob, near, far, spread, keep_row, unit, inv)
     swap = [(0, 1), (1, 0)]
     pair_got = lax.ppermute(pair_send, "seq", swap)
     totals_got = lax.ppermute(totals, "seq", swap)
@@ -306,6 +367,7 @@
     dim = width // heads
     return (
         mesh.shape["seq"] == 2
+        and mesh.shape["res"] == 16
         and keys == 2 * LANES
         and own % 16 == 0
         and depth == 2 * dim

time: 80.1 us -> 44.6 us (0.56)
  waiting for transfers between devices: 47 us -> 21.7 us
  between operations: 14.1 us -> 0.76 us
  starting transfers between devices: 2.06 us -> 9.44 us
  local copies, waits for them, and re-layouts: 8.12 us -> 3.15 us
  Pallas kernels: 8.2 us -> 9.11 us
    all_gather x1 -> x0, waiting for transfers between devices: 42.4 us -> none  [local_gathered(): gathered = lax.all_gather(packed, 'res', axis=0, tiled=True)]
    ppermute x0 -> x5, waiting for transfers between devices: none -> 17.3 us  [swapped(): return lax.ppermute(array, 'res', [(i, i ^ bits) for i in range(parts)])]
    ppermute x0 -> x5, starting transfers between devices: none -> 7.41 us  [swapped(): return lax.ppermute(array, 'res', [(i, i ^ bits) for i in range(parts)])]
    unnamed x20 -> x22, local copies, waits for them, and re-layouts: 8.12 us -> 3.1 us
    pallas_call x0 -> x1, Pallas kernels: none -> 1.04 us  [local_gathered(): call(functools.partial(prepare_kernel, heads), [((3, heads // 2, 2 * LANE...]
  transfers between devices with their start and end apart: 3 -> 7, of which waited for: 2 -> 5; matrix products, arithmetic and copies ran while one was open for 0% -> 0% of each run, Pallas kernels for 0% -> 2%
where the time goes in v2:
time: 44.6 us; the launch traced here: 44.3 us
  waiting for transfers between devices  21.7 us (49%)
  starting transfers between devices  9.44 us (21%)
  Pallas kernels  9.11 us (20%)
  local copies, waits for them, and re-layouts  3.15 us (7%)
  between operations  0.76 us (2%)
    ppermute x5, waiting for transfers between devices, swapped(): return lax.ppermute(array, 'res', [(i, i ^ bits) for i in range(parts)])  17.3 us
    ppermute x5, starting transfers between devices, swapped(): return lax.ppermute(array, 'res', [(i, i ^ bits) for i in range(parts)])  7.41 us
    pallas_call x1, Pallas kernels, local_gathered(): call(functools.partial(main_kernel, heads), [((rows, own, depth), F32), (...  6.09 us
    ppermute x1, waiting for transfers between devices, local_gathered(): pair_got = lax.ppermute(pair_send, 'seq', swap)  4.39 us
    unnamed x22, local copies, waits for them, and re-layouts  3.1 us
    ppermute x1, starting transfers between devices, local_gathered(): totals_got = lax.ppermute(totals, 'seq', swap)  1.49 us
    pallas_call x1, Pallas kernels, local_gathered(): call(last_kernel, [((heads, own, share), F32)] + [((depth, width), F32)]...  1.27 us
    pallas_call x1, Pallas kernels, local_gathered(): call(functools.partial(prepare_kernel, heads), [((3, heads // 2, 2 * LANE...  1.04 us
  transfers between devices with their start and end apart: 7, of which 5 were waited for; matrix products, arithmetic and copies ran while one was open for 0% of the time, Pallas kernels for 2%

profile of v2, /device:TPU:0, one launch (start us, length us, event | category | flops | bytes accessed | tf_op | source)
XLA Modules:
  0.0 44.3 jit_solution(14926342970876591657)
XLA Ops:
  0.6 0.0 copy-start.8
  0.6 0.0 copy-start
  0.7 0.8 %copy-done = bf16[8,16,64]{2,1,0:T(8,128)(2,1)S(1)} copy-done((bf16[8,16,64]{2,1,0:T(8,128)(2,1)S(1)}, bf16[8,16,64]{2,1,0:T(8,128)(2,1)}, u32[]{:S(2)}) %copy-start) | copy-done | bytes 16408
  1.4 0.0 copy-start.2
  1.4 0.8 %copy-done.2 = bf16[8,16,256]{2,1,0:T(8,128)(2,1)S(1)} copy-done((bf16[8,16,256]{2,1,0:T(8,128)(2,1)S(1)}, bf16[8,16,256]{2,1,0:T(8,128)(2,1)}, u32[]{:S(2)}) %copy-start.2) | copy-done | bytes 65560
  2.3 0.8 %copy-done.3 = bf16[8,16,64]{2,1,0:T(8,128)(2,1)S(1)} copy-done((bf16[8,16,64]{2,1,0:T(8,128)(2,1)S(1)}, bf16[8,16,64]{2,1,0:T(8,128)(2,1)}, u32[]{:S(2)}) %copy-start.3) | copy-done | bytes 16408
  3.0 0.7 %copy-done.7 = s32[256]{0:T(256)S(1)} copy-done((s32[256]{0:T(256)S(1)}, s32[256]{0:T(256)}, u32[]{:S(2)}) %copy-start.7) | copy-done | bytes 1048
  3.7 0.7 %shard_map.119 = (bf16[384,128]{1,0:T(8,128)(2,1)S(1)}, f32[8,16,256]{2,1,0:T(8,128)S(1)}) custom-call(bf16[8,16,64]{2,1,0:T(8,128)(2,1)S(1)} %copy-done, bf16[8,16,64]{2,1,0:T(8,128)(2,1)S(1)} %copy-done.3, bf16[8,16,256]{2,1,0:T(8,128)(2,1)S(1)} %copy-done.2, s32[1,256]{1,0:T(1,128)S(1)} %bitcast.10), custom_call_target="tpu_custom_call" | custom-call | tf_op jit(solution)/shard_map/pallas_call | solution.py:312
  4.4 5.1 %collective-permute-start.2 = (bf16[384,128]{1,0:T(8,128)(2,1)S(1)}, bf16[384,128]{1,0:T(8,128)(2,1)S(1)}, u32[]{:S(2)}, u32[]{:S(2)}) collective-permute-start(bf16[384,128]{1,0:T(8,128)(2,1)S(1)} %get-tuple-element.20), channel_id=1, source_target_pairs={{0,24},{2,26},{4,28},{6,30},{8,16},{10,18},{12,20},{14,22},{16,8},... | collective-permute-start | bytes 294920 | tf_op jit(solution)/shard_map/ppermute | solution.py:326
  9.5 0.0 collective-permute-start.1
  9.5 0.6 %collective-permute-start = (bf16[384,128]{1,0:T(8,128)(2,1)S(1)}, bf16[384,128]{1,0:T(8,128)(2,1)S(1)}, u32[]{:S(2)}, u32[]{:S(2)}) collective-permute-start(bf16[384,128]{1,0:T(8,128)(2,1)S(1)} %get-tuple-element.20), channel_id=1, source_target_pairs={{0,8},{2,10},{4,12},{6,14},{8,0},{10,2},{12,4},{14,6},{16,24},{18,... | collective-permute-start | bytes 294920 | tf_op jit(solution)/shard_map/ppermute | solution.py:326
  10.2 3.1 %collective-permute-done.2 = bf16[384,128]{1,0:T(8,128)(2,1)S(1)} collective-permute-done((bf16[384,128]{1,0:T(8,128)(2,1)S(1)}, bf16[384,128]{1,0:T(8,128)(2,1)S(1)}, u32[]{:S(2)}, u32[]{:S(2)}) %collective-permute-start.2) | collective-permute-done | bytes 98336 | tf_op jit(solution)/shard_map/ppermute | solution.py:326
  13.2 4.6 %collective-permute-done.1 = bf16[384,128]{1,0:T(8,128)(2,1)S(1)} collective-permute-done((bf16[384,128]{1,0:T(8,128)(2,1)S(1)}, bf16[384,128]{1,0:T(8,128)(2,1)S(1)}, u32[]{:S(2)}, u32[]{:S(2)}) %collective-permute-start.1) | collective-permute-done | bytes 98336 | tf_op jit(solution)/shard_map/ppermute | solution.py:326
  17.8 0.0 collective-permute-done
  17.8 1.6 %collective-permute-start.3 = (bf16[1536,128]{1,0:T(8,128)(2,1)S(1)}, bf16[1536,128]{1,0:T(8,128)(2,1)S(1)}, u32[]{:S(2)}, u32[]{:S(2)}) collective-permute-start(bf16[1536,128]{1,0:T(8,128)(2,1)S(1)} %pad_maximum_fusion), channel_id=1, source_target_pairs={{0,4},{2,6},{4,0},{6,2},{8,12},{10,14},{12,8},{14,10},{16,20},{18,... | collective-permute-start | bytes 1179656 | tf_op jit(solution)/shard_map/ppermute | solution.py:326
  19.5 8.6 %collective-permute-done.3 = bf16[1536,128]{1,0:T(8,128)(2,1)S(1)} collective-permute-done((bf16[1536,128]{1,0:T(8,128)(2,1)S(1)}, bf16[1536,128]{1,0:T(8,128)(2,1)S(1)}, u32[]{:S(2)}, u32[]{:S(2)}) %collective-permute-start.3) | collective-permute-done | bytes 393248 | tf_op jit(solution)/shard_map/ppermute | solution.py:326
  28.1 0.1 constant_dynamic-update-slice_fusion
  28.1 0.1 collective-permute-start.4
  28.2 0.0 copy-done.8
  28.2 0.0 copy-done.1
  28.2 0.0 copy-done.4
  28.2 0.0 copy-done.5
  28.3 0.0 copy-done.6
  28.3 1.0 %shard_map.120 = (bf16[3,4,256,256]{3,2,1,0:T(8,128)(2,1)S(1)}, f32[1,256]{1,0:T(1,128)S(1)}, f32[8,16,64]{2,1,0:T(8,128)S(1)}, f32[8,16,64]{2,1,0:T(8,128)S(1)}) custom-call(s32[8]{0:T(128)S(1)} %copy-done.8, bf16[8,16,64]{2,1,0:T(8,128)(2,1)S(1)} %copy-done.1, bf16[64,256]{1,0:T(8,128)(2,1)S(1)} %copy-done.4, bf16[64,256]{1,0:T(8,128)(2,1)S(1)} %copy-done.5, ...), custom_call_target="tpu_custom_call" | custom-call | tf_op jit(solution)/shard_map/pallas_call | solution.py:328
  29.3 0.1 pad_add_fusion.where_ref
  29.4 1.1 %collective-permute-done.4 = bf16[3072,128]{1,0:T(8,128)(2,1)S(1)} collective-permute-done((bf16[3072,128]{1,0:T(8,128)(2,1)S(1)}, bf16[3072,128]{1,0:T(8,128)(2,1)S(1)}, u32[]{:S(2)}, u32[]{:S(2)}) %collective-permute-start.4) | collective-permute-done | bytes 786464 | tf_op jit(solution)/shard_map/ppermute | solution.py:326
  30.5 6.1 %shard_map.121 = (f32[8,16,64]{2,1,0:T(8,128)}, f32[9,16,128]{2,1,0:T(8,128)S(1)}, f32[9,16,128]{2,1,0:T(8,128)S(1)}, bf16[192,256]{1,0:T(8,128)(2,1)S(1)}) custom-call(s32[2]{0:T(128)S(1)} %pad_add_fusion.where_ref, f32[8,16,256]{2,1,0:T(8,128)S(1)} %get-tuple-element.19.prob_ref, bf16[8,24,16,128]{3,2,1,0:T(8,128)(2,1)S(1)} %bitcast.7, ...), custom_call_target="tpu_custom_call" | custom-call | tf_op jit(solution)/shard_map/pallas_call | solution.py:343
  36.6 1.5 %collective-permute-start.6 = (bf16[192,256]{1,0:T(8,128)(2,1)S(1)}, bf16[192,256]{1,0:T(8,128)(2,1)S(1)}, u32[]{:S(2)}, u32[]{:S(2)}) collective-permute-start(bf16[192,256]{1,0:T(8,128)(2,1)S(1)} %get-tuple-element.28.totals_ref), channel_id=1, source_target_pairs={{0,1},{1,0},{2,3},{3,2},{4,5},{5,4},{6,7},{7,6},{8,9},{9,8},{10,11... | collective-permute-start | bytes 294920 | tf_op jit(solution)/shard_map/ppermute | solution.py:357
  38.1 0.5 %collective-permute-start.5 = (f32[9,16,128]{2,1,0:T(8,128)S(1)}, f32[9,16,128]{2,1,0:T(8,128)S(1)}, u32[]{:S(2)}, u32[]{:S(2)}) collective-permute-start(f32[9,16,128]{2,1,0:T(8,128)S(1)} %get-tuple-element.27), channel_id=1, source_target_pairs={{0,1},{1,0},{2,3},{3,2},{4,5},{5,4},{6,7},{7,6},{8,9},{9,8},{10,11... | collective-permute-start | bytes 221192 | tf_op jit(solution)/shard_map/ppermute | solution.py:356
  38.6 4.4 %collective-permute-done.5.got_ref = f32[9,16,128]{2,1,0:T(8,128)S(1)} collective-permute-done((f32[9,16,128]{2,1,0:T(8,128)S(1)}, f32[9,16,128]{2,1,0:T(8,128)S(1)}, u32[]{:S(2)}, u32[]{:S(2)}) %collective-permute-start.5) | collective-permute-done | bytes 73760 | tf_op jit(solution)/shard_map/ppermute | solution.py:356
  43.0 0.0 collective-permute-done.6.more_ref
  43.0 1.3 %shard_map.122 = (f32[8,16,128]{2,1,0:T(8,128)}, f32[64,256]{1,0:T(8,128)}, f32[64,256]{1,0:T(8,128)}, f32[64,256]{1,0:T(8,128)}) custom-call(s32[2]{0:T(128)S(1)} %pad_add_fusion.where_ref, f32[8,16,256]{2,1,0:T(8,128)S(1)} %get-tuple-element.19.prob_ref, f32[9,16,128]{2,1,0:T(8,128)S(1)} %get-tuple-element.26.own_ref, ...), custom_call_target="tpu_custom_call" | custom-call | tf_op jit(solution)/shard_map/pallas_call | solution.py:358
  (11 shorter events, 0.1 us)
Async XLA Ops:
  0.6 27.6 %copy-start.8 = (s32[8]{0:T(128)S(1)}, s32[8]{0:T(128)}, u32[]{:S(2)}) copy-start(s32[8]{0:T(128)} %keep_ref.1) | copy-start | bytes 100
  0.6 0.8 %copy-start = (bf16[8,16,64]{2,1,0:T(8,128)(2,1)S(1)}, bf16[8,16,64]{2,1,0:T(8,128)(2,1)}, u32[]{:S(2)}) copy-start(bf16[8,16,64]{2,1,0:T(8,128)(2,1)} %acts_ref.1) | copy-start | bytes 49156
  1.4 0.8 %copy-start.2 = (bf16[8,16,256]{2,1,0:T(8,128)(2,1)S(1)}, bf16[8,16,256]{2,1,0:T(8,128)(2,1)}, u32[]{:S(2)}) copy-start(bf16[8,16,256]{2,1,0:T(8,128)(2,1)} %logits_hbm.1) | copy-start | bytes 196612
  2.2 0.8 %copy-start.3 = (bf16[8,16,64]{2,1,0:T(8,128)(2,1)S(1)}, bf16[8,16,64]{2,1,0:T(8,128)(2,1)}, u32[]{:S(2)}) copy-start(bf16[8,16,64]{2,1,0:T(8,128)(2,1)} %cot_hbm.1) | copy-start | bytes 49156
  3.0 0.7 %copy-start.7 = (s32[256]{0:T(256)S(1)}, s32[256]{0:T(256)}, u32[]{:S(2)}) copy-start(s32[256]{0:T(256)} %param.10) | copy-start | bytes 3076
  3.7 24.5 %copy-start.1 = (bf16[8,16,64]{2,1,0:T(8,128)(2,1)S(1)}, bf16[8,16,64]{2,1,0:T(8,128)(2,1)}, u32[]{:S(2)}) copy-start(bf16[8,16,64]{2,1,0:T(8,128)(2,1)} %acts_ref.1) | copy-start | bytes 49156
  3.7 24.5 %copy-start.4 = (bf16[64,256]{1,0:T(8,128)(2,1)S(1)}, bf16[64,256]{1,0:T(8,128)(2,1)}, u32[]{:S(2)}) copy-start(bf16[64,256]{1,0:T(8,128)(2,1)} %value_ref.1) | copy-start | bytes 98308
  3.7 24.6 %copy-start.5 = (bf16[64,256]{1,0:T(8,128)(2,1)S(1)}, bf16[64,256]{1,0:T(8,128)(2,1)}, u32[]{:S(2)}) copy-start(bf16[64,256]{1,0:T(8,128)(2,1)} %gate_ref.1) | copy-start | bytes 98308
  3.7 24.6 %copy-start.6 = (bf16[256,64]{0,1:T(8,128)(2,1)S(1)}, bf16[256,64]{0,1:T(8,128)(2,1)}, u32[]{:S(2)}) copy-start(bf16[256,64]{0,1:T(8,128)(2,1)} %param.14) | copy-start | bytes 98308
  4.4 8.8 %collective-permute-start.2 = (bf16[384,128]{1,0:T(8,128)(2,1)S(1)}, bf16[384,128]{1,0:T(8,128)(2,1)S(1)}, u32[]{:S(2)}, u32[]{:S(2)}) collective-permute-start(bf16[384,128]{1,0:T(8,128)(2,1)S(1)} %get-tuple-element.20), channel_id=1, source_target_pairs={{0,24},{2,26},{4,28},{6,30},{8,16},{10,18},{12,20},{14,22},{16,8},... | collective-permute-start | bytes 294920 | tf_op jit(solution)/shard_map/ppermute | solution.py:326
  9.5 8.3 %collective-permute-start.1 = (bf16[384,128]{1,0:T(8,128)(2,1)S(1)}, bf16[384,128]{1,0:T(8,128)(2,1)S(1)}, u32[]{:S(2)}, u32[]{:S(2)}) collective-permute-start(bf16[384,128]{1,0:T(8,128)(2,1)S(1)} %get-tuple-element.20), channel_id=1, source_target_pairs={{0,16},{2,18},{4,20},{6,22},{8,24},{10,26},{12,28},{14,30},{16,0},... | collective-permute-start | bytes 294920 | tf_op jit(solution)/shard_map/ppermute | solution.py:326
  9.5 8.3 %collective-permute-start = (bf16[384,128]{1,0:T(8,128)(2,1)S(1)}, bf16[384,128]{1,0:T(8,128)(2,1)S(1)}, u32[]{:S(2)}, u32[]{:S(2)}) collective-permute-start(bf16[384,128]{1,0:T(8,128)(2,1)S(1)} %get-tuple-element.20), channel_id=1, source_target_pairs={{0,8},{2,10},{4,12},{6,14},{8,0},{10,2},{12,4},{14,6},{16,24},{18,... | collective-permute-start | bytes 294920 | tf_op jit(solution)/shard_map/ppermute | solution.py:326
  17.8 10.2 %collective-permute-start.3 = (bf16[1536,128]{1,0:T(8,128)(2,1)S(1)}, bf16[1536,128]{1,0:T(8,128)(2,1)S(1)}, u32[]{:S(2)}, u32[]{:S(2)}) collective-permute-start(bf16[1536,128]{1,0:T(8,128)(2,1)S(1)} %pad_maximum_fusion), channel_id=1, source_target_pairs={{0,4},{2,6},{4,0},{6,2},{8,12},{10,14},{12,8},{14,10},{16,20},{18,... | collective-permute-start | bytes 1179656 | tf_op jit(solution)/shard_map/ppermute | solution.py:326
  28.1 2.4 %collective-permute-start.4 = (bf16[3072,128]{1,0:T(8,128)(2,1)S(1)}, bf16[3072,128]{1,0:T(8,128)(2,1)S(1)}, u32[]{:S(2)}, u32[]{:S(2)}) collective-permute-start(bf16[3072,128]{1,0:T(8,128)(2,1)S(1)} %constant_dynamic-update-slice_fusion), channel_id=1, source_target_pairs={{0,2},{2,0},{4,6},{6,4},{8,10},{10,8},{12,14},{14,12},{16,18},{18,... | collective-permute-start | bytes 2359304 | tf_op jit(solution)/shard_map/ppermute | solution.py:326
  36.6 6.4 %collective-permute-start.6 = (bf16[192,256]{1,0:T(8,128)(2,1)S(1)}, bf16[192,256]{1,0:T(8,128)(2,1)S(1)}, u32[]{:S(2)}, u32[]{:S(2)}) collective-permute-start(bf16[192,256]{1,0:T(8,128)(2,1)S(1)} %get-tuple-element.28.totals_ref), channel_id=1, source_target_pairs={{0,1},{1,0},{2,3},{3,2},{4,5},{5,4},{6,7},{7,6},{8,9},{9,8},{10,11... | collective-permute-start | bytes 294920 | tf_op jit(solution)/shard_map/ppermute | solution.py:357
  38.1 4.9 %collective-permute-start.5 = (f32[9,16,128]{2,1,0:T(8,128)S(1)}, f32[9,16,128]{2,1,0:T(8,128)S(1)}, u32[]{:S(2)}, u32[]{:S(2)}) collective-permute-start(f32[9,16,128]{2,1,0:T(8,128)S(1)} %get-tuple-element.27), channel_id=1, source_target_pairs={{0,1},{1,0},{2,3},{3,2},{4,5},{5,4},{6,7},{7,6},{8,9},{9,8},{10,11... | collective-permute-start | bytes 221192 | tf_op jit(solution)/shard_map/ppermute | solution.py:356

commit v3 on v2

--- a/solution.py
+++ b/solution.py
@@ -42,7 +42,7 @@
 
 
 def pack_kernel(
-    acts_hbm, cot_hbm, logits_hbm, live_hbm, pack_ref, prob_ref,
+    acts_hbm, cot_hbm, logits_hbm, live_hbm, rows_ref, weights_ref, prob_ref,
     acts_ref, cot_ref, logits_ref, live_ref, sems,
 ):
     copies = fetch(
@@ -57,13 +57,13 @@
     unit, _ = standardize(acts_ref[...])
     normed = unit.astype(BF16)
     for b in range(blocks):
-        pack_ref[pl.ds(b * own, own), :] = jnp.concatenate(
+        rows_ref[pl.ds(b * own, own), :] = jnp.concatenate(
             [normed[b * per + k] for k in range(per)], axis=-1
         )
     copies[1].wait()
     cot = cot_ref[...]
     for b in range(blocks):
-        pack_ref[pl.ds((blocks + b) * own, own), :] = jnp.concatenate(
+        rows_ref[pl.ds((blocks + b) * own, own), :] = jnp.concatenate(
             [cot[b * per + k] for k in range(per)], axis=-1
         )
     copies[2].wait()
@@ -76,7 +76,7 @@
         prob_ref[h] = prob
         weights = prob.astype(BF16)
         for w in range(wide):
-            pack_ref[pl.ds((2 * blocks + h * wide + w) * own, own), :] = weights[
+            weights_ref[pl.ds((h * wide + w) * own, own), :] = weights[
                 :, w * LANES : (w + 1) * LANES
             ]
 
@@ -123,50 +123,49 @@
     heads,
     where_ref,
     prob_ref,
-    near_ref,
-    far_ref,
+    near_rows_ref,
+    far_rows_ref,
+    near_weights_ref,
+    far_weights_ref,
     spread_ref,
     keep_row_ref,
-    unit_ref,
-    inv_ref,
-    align_ref,
+    own_grad_ref,
     pair_own_ref,
-    pair_send_ref,
-    totals_ref,
-    all_ref,
+    send_ref,
+    rows_ref,
+    weights_ref,
     att_ref,
     val_grad_ref,
     gate_grad_ref,
 ):
-    rows, own, depth = unit_ref.shape
-    parts, _, _, _ = all_ref.shape
+    parts, blocks, own, _ = rows_ref.shape
+    blocks = blocks // 2
     keys = parts * own
-    dim = keep_row_ref.shape[1] // rows
+    share = keys // 2
+    depth = LANES // 2
+    quad = spread_ref.shape[2] // depth
+    dim = LANES // quad
+    groups = keep_row_ref.shape[1] // LANES
     width = heads * dim
-    quad = LANES // dim
-    groups = rows // quad
-    per = LANES // depth
-    blocks = rows // per
+    span = blocks // groups
     wide = keys // LANES
     first = pl.multiple_of(where_ref[0] * own, own)
     half = where_ref[1]
     for r in range(parts):
         away = where_ref[0] ^ r
-        spot = (away // 2 % 2) * (parts // 4) + away // 4
-        all_ref[r] = jnp.where(away % 2 == 0, near_ref[spot], far_ref[spot])
-
-    def lane_block(k):
-        return all_ref[:, k].reshape(keys, LANES)
-
-    span = quad // per
-    x = [
-        jnp.concatenate([lane_block(g * span + k) for k in range(span)], axis=1)
-        for g in range(groups)
-    ]
-    y = [
-        jnp.concatenate([lane_block(blocks + g * span + k) for k in range(span)], axis=1)
-        for g in range(groups)
-    ]
+        side, column, level = away % 2, away // 2 % 2, away // 4
+        spot = level * 2 + column
+        rows_ref[r] = jnp.where(side == 0, near_rows_ref[spot], far_rows_ref[spot])
+        spot = column * (parts // 4) + level
+        weights_ref[r] = jnp.where(side == 0, near_weights_ref[spot], far_weights_ref[spot])
+
+    def row_block(start):
+        return jnp.concatenate(
+            [rows_ref[:, start + k].reshape(keys, LANES) for k in range(span)], axis=1
+        )
+
+    x = [row_block(g * span) for g in range(groups)]
+    y = [row_block(blocks + g * span) for g in range(groups)]
     x_t = [a.T for a in x]
     y_t = [a.T for a in y]
 
@@ -189,8 +188,13 @@
             out.append(part)
         return out
 
+    def put_pair(h, pair):
+        top = pair.astype(BF16)
+        at = 3 * depth * (width // LANES) + h * own
+        send_ref[pl.ds(at, own), :] = top
+        send_ref[pl.ds(at + (heads + 1) * own, own), :] = (pair - top.astype(F32)).astype(BF16)
+
     folded = [[], [], []]
-    grad_normed = [jnp.zeros((own, quad * depth), F32) for _ in range(groups)]
     sums = jnp.zeros((own, LANES), F32)
     for p in range(heads // 2):
         value_bd = spread_ref[0, p]
@@ -204,7 +208,7 @@
             h = 2 * p + k
             cut = slice(k * LANES, (k + 1) * LANES)
             weights = jnp.concatenate(
-                [lane_block(2 * blocks + h * wide + w) for w in range(wide)], axis=1
+                [weights_ref[:, h * wide + w].reshape(keys, LANES) for w in range(wide)], axis=1
             )
             vals = jnp.concatenate([v[:, cut] for v in values], axis=1)
             attended = dot(weights, vals)
@@ -222,7 +226,7 @@
             sums = jnp.where(lane == h, jnp.sum(prob * pair, axis=-1, keepdims=True), sums)
             low, high = pair[:, : keys // 2], pair[:, keys // 2 :]
             pair_own_ref[h] = jnp.where(half == 0, low, high)
-            pair_send_ref[h] = jnp.where(half == 0, high, low)
+            put_pair(h, jnp.where(half == 0, high, low))
         totals = [None, None, None]
         for g in range(groups):
             cut = slice(g * LANES, (g + 1) * LANES)
@@ -231,53 +235,69 @@
             vg = jnp.concatenate([a[:, cut] for a in val_grad], axis=1)
             gate_grad_ref[p * groups + g] = gg
             val_grad_ref[p * groups + g] = vg
-            grad_normed[g] = (
-                grad_normed[g]
-                + dot_nt(val_grad_ref[p * groups + g, pl.ds(first, own), :], value_bd)
-                + dot_nt(gate_grad_ref[p * groups + g, pl.ds(first, own), :], gate_bd)
-            )
+            own_grad_ref[0, p * groups + g] = val_grad_ref[p * groups + g, pl.ds(first, own), :]
+            own_grad_ref[1, p * groups + g] = gate_grad_ref[p * groups + g, pl.ds(first, own), :]
             for t, (left, right) in enumerate(((x_t, vg), (x_t, gg), (y_t, mo))):
                 term = dot(left[g], right)
                 totals[t] = term if totals[t] is None else totals[t] + term
         for t in range(3):
             folded[t].extend(fold(totals[t]))
 
-    pair_send_ref[heads] = sums
+    put_pair(heads, sums)
     pair_own_ref[heads] = sums
     for t in range(3):
-        cols = []
         for b in range(width // LANES):
             block = folded[t][b * quad]
             for k in range(1, quad):
                 block = jnp.where(slot == k, folded[t][b * quad + k], block)
-            cols.append(block)
-        totals_ref[pl.ds(t * depth, depth), :] = jnp.concatenate(cols, axis=1).astype(BF16)
-
-    for s in range(rows):
-        g, k = divmod(s, quad)
-        grad = grad_normed[g][:, k * depth : (k + 1) * depth]
-        lead = jnp.mean(grad, axis=-1, keepdims=True)
-        trail = jnp.mean(grad * unit_ref[s], axis=-1, keepdims=True)
-        align_ref[s] = inv_ref[s] * (grad - lead - unit_ref[s] * trail)
+            at = (t * (width // LANES) + b) * depth
+            send_ref[pl.ds(at, depth), :] = block.astype(BF16)
+
+
+def align_kernel(spread_ref, unit_ref, inv_ref, own_grad_ref, align_ref):
+    rows, own, depth = unit_ref.shape
+    pairs = spread_ref.shape[1]
+    groups = own_grad_ref.shape[1] // pairs
+    quad = rows // groups
+    for g in range(groups):
+        total = jnp.zeros((own, quad * depth), F32)
+        for p in range(pairs):
+            for t in range(2):
+                total = total + dot_nt(own_grad_ref[t, p * groups + g], spread_ref[t, p])
+        for k in range(quad):
+            s = g * quad + k
+            grad = total[:, k * depth : (k + 1) * depth]
+            lead = jnp.mean(grad, axis=-1, keepdims=True)
+            trail = jnp.mean(grad * unit_ref[s], axis=-1, keepdims=True)
+            align_ref[s] = inv_ref[s] * (grad - lead - unit_ref[s] * trail)
 
 
 def last_kernel(
-    where_ref, prob_ref, own_ref, got_ref, totals_ref, more_ref, pair_ref, value_ref, gate_ref, output_ref
-):
-    heads = prob_ref.shape[0]
-    share = own_ref.shape[2]
+    where_ref, prob_ref, own_ref, mine_ref, got_ref, pair_ref, value_ref, gate_ref, output_ref
+):
+    heads, own, keys = prob_ref.shape
+    share = keys // 2
+    depth, width = value_ref.shape
     half = where_ref[1]
-    sums = own_ref[heads] + got_ref[heads]
+
+    def got_pair(h):
+        at = 3 * depth * (width // LANES) + h * own
+        top = got_ref[pl.ds(at, own), :].astype(F32)
+        return top + got_ref[pl.ds(at + (heads + 1) * own, own), :].astype(F32)
+
+    sums = own_ref[heads] + got_pair(heads)
     for h in range(heads):
         prob = jnp.where(half == 0, prob_ref[h, :, :share], prob_ref[h, :, share:])
-        pair_ref[h] = prob * (own_ref[h] + got_ref[h] - sums[:, h : h + 1])
-    depth = value_ref.shape[0]
+        pair_ref[h] = prob * (own_ref[h] + got_pair(h) - sums[:, h : h + 1])
     for t, ref in enumerate((value_ref, gate_ref, output_ref)):
-        rows = pl.ds(t * depth, depth)
-        ref[...] = totals_ref[rows, :].astype(F32) + more_ref[rows, :].astype(F32)
-
-
-def call(kernel, outs, spaces, scratch=()):
+        for b in range(width // LANES):
+            at = pl.ds((t * (width // LANES) + b) * depth, depth)
+            ref[:, b * LANES : (b + 1) * LANES] = mine_ref[at, :].astype(F32) + got_ref[
+                at, :
+            ].astype(F32)
+
+
+def call(kernel, outs, spaces, scratch=(), limit=16 * 1024 * 1024, cost=None):
     spec = {
         "v": pl.BlockSpec(memory_space=pltpu.VMEM),
         "s": pl.BlockSpec(memory_space=pltpu.SMEM),
@@ -289,7 +309,8 @@
         in_specs=[spec[c] for c in spaces],
         out_specs=[spec["v"]] * len(outs),
         scratch_shapes=list(scratch),
-        compiler_params=pltpu.CompilerParams(vmem_limit_bytes=48 * 1024 * 1024),
+        compiler_params=pltpu.CompilerParams(vmem_limit_bytes=limit),
+        cost_estimate=cost,
     )
 
 
@@ -307,11 +328,17 @@
     heads, _, keys = pair_head_logits.shape
     width = value_matrix.shape[1]
     parts = keys // own
-    lanes = (2 * rows * depth + heads * keys) // LANES
+    row_blocks = 2 * rows * depth // LANES
+    weight_blocks = heads * keys // LANES
+    share = keys // 2
     where = jnp.stack([lax.axis_index("res"), lax.axis_index("seq")]).astype(jnp.int32)
-    packed, prob = call(
+    packed_rows, packed_weights, prob = call(
         pack_kernel,
-        [((lanes * own, LANES), BF16), ((heads, own, keys), F32)],
+        [
+            ((row_blocks * own, LANES), BF16),
+            ((weight_blocks * own, LANES), BF16),
+            ((heads, own, keys), F32),
+        ],
         "hhhh",
         [
             pltpu.VMEM((rows, own, depth), BF16),
@@ -320,10 +347,14 @@
             pltpu.VMEM((1, keys), jnp.int32),
             pltpu.SemaphoreType.DMA((4,)),
         ],
+        None,
     )(alignment_activations, cotangent, pair_head_logits, residue_mask.reshape(1, keys))
 
     def swapped(array, bits):
         return lax.ppermute(array, "res", [(i, i ^ bits) for i in range(parts)])
+
+    def line(array):
+        return jnp.concatenate([array] + [swapped(array, 4 * k) for k in range(1, parts // 4)])
 
     spread, keep_row, unit, inv = call(
         functools.partial(prepare_kernel, heads),
@@ -335,31 +366,47 @@
         ],
         "svvvv",
     )(alignment_row_mask, alignment_activations, value_matrix, gate_matrix, output_matrix.T)
-    line = jnp.concatenate([packed] + [swapped(packed, 4 * k) for k in range(1, parts // 4)])
-    plane = jnp.concatenate([line, swapped(line, 2)])
-    other = swapped(plane, 1)
-    near, far = (a.reshape(parts // 2, lanes, own, LANES) for a in (plane, other))
-    share = keys // 2
-    align, pair_own, pair_send, totals = call(
+    weights_line = line(packed_weights)
+    rows_pair = jnp.concatenate([packed_rows, swapped(packed_rows, 2)])
+    weights_plane = jnp.concatenate([weights_line, swapped(weights_line, 2)])
+    rows_plane = line(rows_pair)
+
+    def split(array, blocks):
+        return array.reshape(parts // 2, blocks, own, LANES)
+
+    own_grad, pair_own, send = call(
         functools.partial(main_kernel, heads),
         [
-            ((rows, own, depth), F32),
+            ((2, heads // 2 * rows * width // heads // LANES, own, 2 * LANES), BF16),
             ((heads + 1, own, share), F32),
-            ((heads + 1, own, share), F32),
-            ((3 * depth, width), BF16),
+            ((3 * depth * width // LANES + 2 * (heads + 1) * own, LANES), BF16),
         ],
         "svvvvvvv",
-        [pltpu.VMEM((parts, lanes, own, LANES), BF16)]
+        [
+            pltpu.VMEM((parts, row_blocks, own, LANES), BF16),
+            pltpu.VMEM((parts, weight_blocks, own, LANES), BF16),
+        ]
         + [pltpu.VMEM((heads, keys, 2 * LANES), BF16)] * 3,
-    )(where, prob, near, far, spread, keep_row, unit, inv)
-    swap = [(0, 1), (1, 0)]
-    pair_got = lax.ppermute(pair_send, "seq", swap)
-    totals_got = lax.ppermute(totals, "seq", swap)
+        32 * 1024 * 1024,
+    )(
+        where,
+        prob,
+        split(rows_plane, row_blocks),
+        split(swapped(rows_plane, 1), row_blocks),
+        split(weights_plane, weight_blocks),
+        split(swapped(weights_plane, 1), weight_blocks),
+        spread,
+        keep_row,
+    )
+    got = lax.ppermute(send, "seq", [(0, 1), (1, 0)])
+    (align,) = call(align_kernel, [((rows, own, depth), F32)], "vvvv")(
+        spread, unit, inv, own_grad
+    )
     pair, value_total, gate_total, output_total = call(
         last_kernel,
         [((heads, own, share), F32)] + [((depth, width), F32)] * 3,
-        "svvvvv",
-    )(where, prob, pair_own, pair_got, totals, totals_got)
+        "svvvv",
+    )(where, prob, pair_own, send, got)
     return align, pair, value_total, gate_total, output_total.T
 
 

time: 44.6 us -> 39.7 us (0.89)
  waiting for transfers between devices: 21.7 us -> 8.91 us
  starting transfers between devices: 9.44 us -> 16 us
  Pallas kernels: 9.11 us -> 10.9 us
  local copies, waits for them, and re-layouts: 3.15 us -> 1.8 us
  other arithmetic: 0.1 us -> 0.94 us
    ppermute x5 -> x10, waiting for transfers between devices: 17.3 us -> 5.83 us  [swapped(): return lax.ppermute(array, 'res', [(i, i ^ bits) for i in range(parts)])]
    ppermute x5 -> x10, starting transfers between devices: 7.41 us -> 14.3 us  [swapped(): return lax.ppermute(array, 'res', [(i, i ^ bits) for i in range(parts)])]
    pallas_call x2 -> x3, Pallas kernels: 6.81 us -> 8.54 us  [the longest x1 4.91 us: local_gathered(): call(functools.partial(main_kernel, heads), [((2, heads // 2 * rows * wid...]
    unnamed x22 -> x19, local copies, waits for them, and re-layouts: 3.1 us -> 1.74 us
    ppermute x2 -> x1, waiting for transfers between devices: 4.39 us -> 3.08 us  [local_gathered(): got = lax.ppermute(send, 'seq', [(0, 1), (1, 0)])]
    concatenate x1, other arithmetic: 0.03 us -> 0.86 us  [line(): jnp.concatenate([array] + [swapped(array, 4 * k) for k in range(1, parts...]
    ppermute x2 -> x1, starting transfers between devices: 2.03 us -> 1.77 us  [local_gathered(): got = lax.ppermute(send, 'seq', [(0, 1), (1, 0)])]
  transfers between devices with their start and end apart: 7 -> 11, of which waited for: 5 -> 4; matrix products, arithmetic and copies ran while one was open for 0% -> 7% of each run, Pallas kernels for 2% -> 7%
where the time goes in v3:
time: 39.7 us; the launch traced here: 39.4 us
  starting transfers between devices  16 us (40%)
  Pallas kernels  10.9 us (27%)
  waiting for transfers between devices  8.91 us (22%)
  local copies, waits for them, and re-layouts  1.8 us (5%)
  other arithmetic  0.94 us (2%)
  between operations  0.8 us (2%)
    ppermute x10, starting transfers between devices, swapped(): return lax.ppermute(array, 'res', [(i, i ^ bits) for i in range(parts)])  14.3 us
    ppermute x10, waiting for transfers between devices, swapped(): return lax.ppermute(array, 'res', [(i, i ^ bits) for i in range(parts)])  5.83 us
    pallas_call x1, Pallas kernels, local_gathered(): call(functools.partial(main_kernel, heads), [((2, heads // 2 * rows * wid...  4.91 us
    ppermute x1, waiting for transfers between devices, local_gathered(): got = lax.ppermute(send, 'seq', [(0, 1), (1, 0)])  3.08 us
    pallas_call x1, Pallas kernels, local_gathered(): call(pack_kernel, [((row_blocks * own, LANES), BF16), ((weight_blocks * o...  2 us
    ppermute x1, starting transfers between devices, local_gathered(): got = lax.ppermute(send, 'seq', [(0, 1), (1, 0)])  1.77 us
    unnamed x19, local copies, waits for them, and re-layouts  1.74 us
    pallas_call x1, Pallas kernels, local_gathered(): call(align_kernel, [((rows, own, depth), F32)], 'vvvv')  1.63 us
  transfers between devices with their start and end apart: 11, of which 4 were waited for; matrix products, arithmetic and copies ran while one was open for 7% of the time, Pallas kernels for 7%

profile of v3, /device:TPU:0, one launch (start us, length us, event | category | flops | bytes accessed | tf_op | source)
XLA Modules:
  0.0 39.4 jit_solution(4308236829905705728)
XLA Ops:
  0.7 2.0 %shard_map.120 = (bf16[128,128]{1,0:T(8,128)(2,1)}, bf16[256,128]{1,0:T(8,128)(2,1)}, f32[8,16,256]{2,1,0:T(8,128)}) custom-call(bf16[8,16,64]{2,1,0:T(8,128)(2,1)} %acts_hbm.1, bf16[8,16,64]{2,1,0:T(8,128)(2,1)} %cot_hbm.1, bf16[8,16,256]{2,1,0:T(8,128)(2,1)} %logits_hbm.1, s32[1,256]{1,0:T(1,128)} %bitcast.14), custom_call_target="tpu_custom_call" | custom-call | tf_op jit(solution)/shard_map/pallas_call | solution.py:335
  2.7 3.1 %collective-permute-start.5 = (bf16[256,128]{1,0:T(8,128)(2,1)}, bf16[256,128]{1,0:T(8,128)(2,1)S(1)}, u32[]{:S(2)}, u32[]{:S(2)}) collective-permute-start(bf16[256,128]{1,0:T(8,128)(2,1)} %get-tuple-element.24), channel_id=1, source_target_pairs={{0,8},{2,10},{4,12},{6,14},{8,0},{10,2},{12,4},{14,6},{16,24},{18,... | collective-permute-start | bytes 196616 | tf_op jit(solution)/shard_map/ppermute | solution.py:354
  5.8 2.6 %collective-permute-start.6 = (bf16[256,128]{1,0:T(8,128)(2,1)}, bf16[256,128]{1,0:T(8,128)(2,1)S(1)}, u32[]{:S(2)}, u32[]{:S(2)}) collective-permute-start(bf16[256,128]{1,0:T(8,128)(2,1)} %get-tuple-element.24), channel_id=1, source_target_pairs={{0,16},{2,18},{4,20},{6,22},{8,24},{10,26},{12,28},{14,30},{16,0},... | collective-permute-start | bytes 196616 | tf_op jit(solution)/shard_map/ppermute | solution.py:354
  8.4 0.0 collective-permute-start.7
  8.4 1.7 %collective-permute-start = (bf16[128,128]{1,0:T(8,128)(2,1)}, bf16[128,128]{1,0:T(8,128)(2,1)S(1)}, u32[]{:S(2)}, u32[]{:S(2)}) collective-permute-start(bf16[128,128]{1,0:T(8,128)(2,1)} %get-tuple-element.23), channel_id=1, source_target_pairs={{0,4},{2,6},{4,0},{6,2},{8,12},{10,14},{12,8},{14,10},{16,20},{18,... | collective-permute-start | bytes 98312 | tf_op jit(solution)/shard_map/ppermute | solution.py:354
  10.1 0.8 %constant_dynamic-update-slice_fusion.1 = (bf16[256,128]{1,0:T(8,128)(2,1)S(1)}, bf16[1024,128]{1,0:T(8,128)(2,1)S(1)}) fusion(bf16[128,128]{1,0:T(8,128)(2,1)} %get-tuple-element.23), kind=kLoop, calls=%fused_computation.2 | loop fusion | bytes 98304
  10.9 0.8 %constant_dynamic-update-slice_fusion.11 = bf16[2048,128]{1,0:T(8,128)(2,1)S(1)} fusion(bf16[256,128]{1,0:T(8,128)(2,1)} %get-tuple-element.24), kind=kLoop, calls=%fused_computation.12 | loop fusion | bytes 131072
  11.8 0.7 %collective-permute-done = bf16[128,128]{1,0:T(8,128)(2,1)S(1)} collective-permute-done((bf16[128,128]{1,0:T(8,128)(2,1)}, bf16[128,128]{1,0:T(8,128)(2,1)S(1)}, u32[]{:S(2)}, u32[]{:S(2)}) %collective-permute-start) | collective-permute-done | bytes 32800 | tf_op jit(solution)/shard_map/ppermute | solution.py:354
  12.5 1.0 %collective-permute-start.1 = (bf16[256,128]{1,0:T(8,128)(2,1)S(1)}, bf16[256,128]{1,0:T(8,128)(2,1)S(1)}, u32[]{:S(2)}, u32[]{:S(2)}) collective-permute-start(bf16[256,128]{1,0:T(8,128)(2,1)S(1)} %get-tuple-element.33), channel_id=1, source_target_pairs={{0,8},{2,10},{4,12},{6,14},{8,0},{10,2},{12,4},{14,6},{16,24},{18,... | collective-permute-start | bytes 196616 | tf_op jit(solution)/shard_map/ppermute | solution.py:354
  13.5 3.5 %collective-permute-start.2 = (bf16[256,128]{1,0:T(8,128)(2,1)S(1)}, bf16[256,128]{1,0:T(8,128)(2,1)S(1)}, u32[]{:S(2)}, u32[]{:S(2)}) collective-permute-start(bf16[256,128]{1,0:T(8,128)(2,1)S(1)} %get-tuple-element.33), channel_id=1, source_target_pairs={{0,16},{2,18},{4,20},{6,22},{8,24},{10,26},{12,28},{14,30},{16,0},... | collective-permute-start | bytes 196616 | tf_op jit(solution)/shard_map/ppermute | solution.py:354
  17.0 0.0 collective-permute-done.5
  17.0 0.0 collective-permute-start.3
  17.0 0.0 collective-permute-done.6
  17.0 0.0 collective-permute-done.7
  17.0 0.9 %pad_maximum_fusion = bf16[1024,128]{1,0:T(8,128)(2,1)S(1)} fusion(bf16[256,128]{1,0:T(8,128)(2,1)S(1)} %collective-permute-done.7, bf16[256,128]{1,0:T(8,128)(2,1)S(1)} %collective-permute-done.6, bf16[256,128]{1,0:T(8,128)(2,1)S(1)} %collective-permute-done.5, bf16[256,128]{1,0:T(8,128)(2,1)} %get-tuple-element.24), kind=kLoop, calls=%fused_computation | loop fusion | flops 1048576 | bytes 524288 | tf_op jit(solution)/shard_map/concatenate | solution.py:357
  17.9 1.8 %collective-permute-start.8 = (bf16[1024,128]{1,0:T(8,128)(2,1)S(1)}, bf16[1024,128]{1,0:T(8,128)(2,1)S(1)}, u32[]{:S(2)}, u32[]{:S(2)}) collective-permute-start(bf16[1024,128]{1,0:T(8,128)(2,1)S(1)} %pad_maximum_fusion), channel_id=1, source_target_pairs={{0,4},{2,6},{4,0},{6,2},{8,12},{10,14},{12,8},{14,10},{16,20},{18,... | collective-permute-start | bytes 786440 | tf_op jit(solution)/shard_map/ppermute | solution.py:354
  19.7 4.6 %collective-permute-done.8 = bf16[1024,128]{1,0:T(8,128)(2,1)S(1)} collective-permute-done((bf16[1024,128]{1,0:T(8,128)(2,1)S(1)}, bf16[1024,128]{1,0:T(8,128)(2,1)S(1)}, u32[]{:S(2)}, u32[]{:S(2)}) %collective-permute-start.8) | collective-permute-done | bytes 262176 | tf_op jit(solution)/shard_map/ppermute | solution.py:354
  24.3 0.1 collective-permute-start.9
  24.4 0.0 collective-permute-done.1
  24.4 0.0 collective-permute-done.2
  24.5 0.0 collective-permute-done.3
  24.5 0.5 %collective-permute-start.4 = (bf16[1024,128]{1,0:T(8,128)(2,1)S(1)}, bf16[1024,128]{1,0:T(8,128)(2,1)S(1)}, u32[]{:S(2)}, u32[]{:S(2)}) collective-permute-start(bf16[1024,128]{1,0:T(8,128)(2,1)S(1)} %constant_dynamic-update-slice_fusion.2), channel_id=1, source_target_pairs={{0,2},{2,0},{4,6},{6,4},{8,10},{10,8},{12,14},{14,12},{16,18},{18,... | collective-permute-start | bytes 786440 | tf_op jit(solution)/shard_map/ppermute | solution.py:354
  25.1 0.0 copy-done.3
  25.1 1.0 %shard_map.119 = (bf16[3,4,256,256]{3,2,1,0:T(8,128)(2,1)S(1)}, f32[1,256]{1,0:T(1,128)S(1)}, f32[8,16,64]{2,1,0:T(8,128)S(1)}, f32[8,16,64]{2,1,0:T(8,128)S(1)}) custom-call(s32[8]{0:T(128)S(1)} %copy-done.5, bf16[8,16,64]{2,1,0:T(8,128)(2,1)S(1)} %copy-done.1, bf16[64,256]{1,0:T(8,128)(2,1)S(1)} %copy-done.2, bf16[64,256]{1,0:T(8,128)(2,1)S(1)} %copy-done.3, ...), custom_call_target="tpu_custom_call" | custom-call | tf_op jit(solution)/shard_map/pallas_call | solution.py:359
  26.1 0.1 pad_add_fusion.where_ref
  26.2 0.5 %collective-permute-done.4 = bf16[1024,128]{1,0:T(8,128)(2,1)S(1)} collective-permute-done((bf16[1024,128]{1,0:T(8,128)(2,1)S(1)}, bf16[1024,128]{1,0:T(8,128)(2,1)S(1)}, u32[]{:S(2)}, u32[]{:S(2)}) %collective-permute-start.4) | collective-permute-done | bytes 262176 | tf_op jit(solution)/shard_map/ppermute | solution.py:354
  26.7 0.0 collective-permute-done.9
  26.7 4.9 %shard_map.121 = (bf16[2,8,16,256]{3,2,1,0:T(8,128)(2,1)S(1)}, f32[9,16,128]{2,1,0:T(8,128)S(1)}, bf16[672,128]{1,0:T(8,128)(2,1)S(1)}) custom-call(s32[2]{0:T(128)S(1)} %pad_add_fusion.where_ref, f32[8,16,256]{2,1,0:T(8,128)S(1)} %copy-done, bf16[8,8,16,128]{3,2,1,0:T(8,128)(2,1)S(1)} %bitcast.11, bf16[8,8,16,128]{3,2,1,0:T(8,128)(2,1)S(1)} %bitcast.12, ...), custom_call_target="tpu_custom_call" | custom-call | tf_op jit(solution)/shard_map/pallas_call | solution.py:377
  31.6 1.8 %collective-permute-start.10 = (bf16[672,128]{1,0:T(8,128)(2,1)S(1)}, bf16[672,128]{1,0:T(8,128)(2,1)S(1)}, u32[]{:S(2)}, u32[]{:S(2)}) collective-permute-start(bf16[672,128]{1,0:T(8,128)(2,1)S(1)} %get-tuple-element.28.mine_ref), channel_id=1, source_target_pairs={{0,1},{1,0},{2,3},{3,2},{4,5},{5,4},{6,7},{7,6},{8,9},{9,8},{10,11... | collective-permute-start | bytes 516104 | tf_op jit(solution)/shard_map/ppermute | solution.py:401
  33.4 1.6 %shard_map.122 = f32[8,16,64]{2,1,0:T(8,128)} custom-call(bf16[3,4,256,256]{3,2,1,0:T(8,128)(2,1)S(1)} %get-tuple-element.19.spread_ref, f32[8,16,64]{2,1,0:T(8,128)S(1)} %get-tuple-element.20.unit_ref, f32[8,16,64]{2,1,0:T(8,128)S(1)} %get-tuple-element.21.inv_ref, bf16[2,8,16,256]{3,2,1,0:T(8,128)(2,1)S(1)} %get-tuple-element.26.own_grad_ref), custom_call_target="tpu_custom_call" | custom-call | tf_op jit(solution)/shard_map/pallas_call | solution.py:402
  35.0 3.1 %collective-permute-done.10.got_ref = bf16[672,128]{1,0:T(8,128)(2,1)S(1)} collective-permute-done((bf16[672,128]{1,0:T(8,128)(2,1)S(1)}, bf16[672,128]{1,0:T(8,128)(2,1)S(1)}, u32[]{:S(2)}, u32[]{:S(2)}) %collective-permute-start.10) | collective-permute-done | bytes 172064 | tf_op jit(solution)/shard_map/ppermute | solution.py:401
  38.1 1.3 %shard_map.123 = (f32[8,16,128]{2,1,0:T(8,128)}, f32[64,256]{1,0:T(8,128)}, f32[64,256]{1,0:T(8,128)}, f32[64,256]{1,0:T(8,128)}) custom-call(s32[2]{0:T(128)S(1)} %pad_add_fusion.where_ref, f32[8,16,256]{2,1,0:T(8,128)S(1)} %copy-done, f32[9,16,128]{2,1,0:T(8,128)S(1)} %get-tuple-element.27.own_ref, bf16[672,128]{1,0:T(8,128)(2,1)S(1)} %get-tuple-element.28.mine_ref, ...), custom_call_target="tpu_custom_call" | custom-call | tf_op jit(solution)/shard_map/pallas_call | solution.py:405
  (19 shorter events, 0.2 us)
Async XLA Ops:
  0.6 24.4 %copy-start.1 = (bf16[8,16,64]{2,1,0:T(8,128)(2,1)S(1)}, bf16[8,16,64]{2,1,0:T(8,128)(2,1)}, u32[]{:S(2)}) copy-start(bf16[8,16,64]{2,1,0:T(8,128)(2,1)} %acts_hbm.1) | copy-start | bytes 49156
  0.6 24.4 %copy-start.5 = (s32[8]{0:T(128)S(1)}, s32[8]{0:T(128)}, u32[]{:S(2)}) copy-start(s32[8]{0:T(128)} %keep_ref.1) | copy-start | bytes 100
  0.7 24.4 %copy-start.2 = (bf16[64,256]{1,0:T(8,128)(2,1)S(1)}, bf16[64,256]{1,0:T(8,128)(2,1)}, u32[]{:S(2)}) copy-start(bf16[64,256]{1,0:T(8,128)(2,1)} %value_ref.1) | copy-start | bytes 98308
  0.7 24.4 %copy-start.3 = (bf16[64,256]{1,0:T(8,128)(2,1)S(1)}, bf16[64,256]{1,0:T(8,128)(2,1)}, u32[]{:S(2)}) copy-start(bf16[64,256]{1,0:T(8,128)(2,1)} %gate_ref.1) | copy-start | bytes 98308
  0.7 24.4 %copy-start.4 = (bf16[256,64]{0,1:T(8,128)(2,1)S(1)}, bf16[256,64]{0,1:T(8,128)(2,1)}, u32[]{:S(2)}) copy-start(bf16[256,64]{0,1:T(8,128)(2,1)} %param.14) | copy-start | bytes 98308
  2.7 24.0 %copy-start = (f32[8,16,256]{2,1,0:T(8,128)S(1)}, f32[8,16,256]{2,1,0:T(8,128)}, u32[]{:S(2)}) copy-start(f32[8,16,256]{2,1,0:T(8,128)} %get-tuple-element.22.prob_ref) | copy-start | bytes 393220
  2.7 14.3 %collective-permute-start.5 = (bf16[256,128]{1,0:T(8,128)(2,1)}, bf16[256,128]{1,0:T(8,128)(2,1)S(1)}, u32[]{:S(2)}, u32[]{:S(2)}) collective-permute-start(bf16[256,128]{1,0:T(8,128)(2,1)} %get-tuple-element.24), channel_id=1, source_target_pairs={{0,8},{2,10},{4,12},{6,14},{8,0},{10,2},{12,4},{14,6},{16,24},{18,... | collective-permute-start | bytes 196616 | tf_op jit(solution)/shard_map/ppermute | solution.py:354
  5.8 11.2 %collective-permute-start.6 = (bf16[256,128]{1,0:T(8,128)(2,1)}, bf16[256,128]{1,0:T(8,128)(2,1)S(1)}, u32[]{:S(2)}, u32[]{:S(2)}) collective-permute-start(bf16[256,128]{1,0:T(8,128)(2,1)} %get-tuple-element.24), channel_id=1, source_target_pairs={{0,16},{2,18},{4,20},{6,22},{8,24},{10,26},{12,28},{14,30},{16,0},... | collective-permute-start | bytes 196616 | tf_op jit(solution)/shard_map/ppermute | solution.py:354
  8.4 8.6 %collective-permute-start.7 = (bf16[256,128]{1,0:T(8,128)(2,1)}, bf16[256,128]{1,0:T(8,128)(2,1)S(1)}, u32[]{:S(2)}, u32[]{:S(2)}) collective-permute-start(bf16[256,128]{1,0:T(8,128)(2,1)} %get-tuple-element.24), channel_id=1, source_target_pairs={{0,24},{2,26},{4,28},{6,30},{8,16},{10,18},{12,20},{14,22},{16,8},... | collective-permute-start | bytes 196616 | tf_op jit(solution)/shard_map/ppermute | solution.py:354
  8.4 4.1 %collective-permute-start = (bf16[128,128]{1,0:T(8,128)(2,1)}, bf16[128,128]{1,0:T(8,128)(2,1)S(1)}, u32[]{:S(2)}, u32[]{:S(2)}) collective-permute-start(bf16[128,128]{1,0:T(8,128)(2,1)} %get-tuple-element.23), channel_id=1, source_target_pairs={{0,4},{2,6},{4,0},{6,2},{8,12},{10,14},{12,8},{14,10},{16,20},{18,... | collective-permute-start | bytes 98312 | tf_op jit(solution)/shard_map/ppermute | solution.py:354
  12.5 11.9 %collective-permute-start.1 = (bf16[256,128]{1,0:T(8,128)(2,1)S(1)}, bf16[256,128]{1,0:T(8,128)(2,1)S(1)}, u32[]{:S(2)}, u32[]{:S(2)}) collective-permute-start(bf16[256,128]{1,0:T(8,128)(2,1)S(1)} %get-tuple-element.33), channel_id=1, source_target_pairs={{0,8},{2,10},{4,12},{6,14},{8,0},{10,2},{12,4},{14,6},{16,24},{18,... | collective-permute-start | bytes 196616 | tf_op jit(solution)/shard_map/ppermute | solution.py:354
  13.5 11.0 %collective-permute-start.2 = (bf16[256,128]{1,0:T(8,128)(2,1)S(1)}, bf16[256,128]{1,0:T(8,128)(2,1)S(1)}, u32[]{:S(2)}, u32[]{:S(2)}) collective-permute-start(bf16[256,128]{1,0:T(8,128)(2,1)S(1)} %get-tuple-element.33), channel_id=1, source_target_pairs={{0,16},{2,18},{4,20},{6,22},{8,24},{10,26},{12,28},{14,30},{16,0},... | collective-permute-start | bytes 196616 | tf_op jit(solution)/shard_map/ppermute | solution.py:354
  17.0 7.5 %collective-permute-start.3 = (bf16[256,128]{1,0:T(8,128)(2,1)S(1)}, bf16[256,128]{1,0:T(8,128)(2,1)S(1)}, u32[]{:S(2)}, u32[]{:S(2)}) collective-permute-start(bf16[256,128]{1,0:T(8,128)(2,1)S(1)} %get-tuple-element.33), channel_id=1, source_target_pairs={{0,24},{2,26},{4,28},{6,30},{8,16},{10,18},{12,20},{14,22},{16,8},... | collective-permute-start | bytes 196616 | tf_op jit(solution)/shard_map/ppermute | solution.py:354
  17.9 6.4 %collective-permute-start.8 = (bf16[1024,128]{1,0:T(8,128)(2,1)S(1)}, bf16[1024,128]{1,0:T(8,128)(2,1)S(1)}, u32[]{:S(2)}, u32[]{:S(2)}) collective-permute-start(bf16[1024,128]{1,0:T(8,128)(2,1)S(1)} %pad_maximum_fusion), channel_id=1, source_target_pairs={{0,4},{2,6},{4,0},{6,2},{8,12},{10,14},{12,8},{14,10},{16,20},{18,... | collective-permute-start | bytes 786440 | tf_op jit(solution)/shard_map/ppermute | solution.py:354
  24.3 2.4 %collective-permute-start.9 = (bf16[2048,128]{1,0:T(8,128)(2,1)S(1)}, bf16[2048,128]{1,0:T(8,128)(2,1)S(1)}, u32[]{:S(2)}, u32[]{:S(2)}) collective-permute-start(bf16[2048,128]{1,0:T(8,128)(2,1)S(1)} %constant_dynamic-update-slice_fusion.7), channel_id=1, source_target_pairs={{0,2},{2,0},{4,6},{6,4},{8,10},{10,8},{12,14},{14,12},{16,18},{18,... | collective-permute-start | bytes 1572872 | tf_op jit(solution)/shard_map/ppermute | solution.py:354
  24.5 2.2 %collective-permute-start.4 = (bf16[1024,128]{1,0:T(8,128)(2,1)S(1)}, bf16[1024,128]{1,0:T(8,128)(2,1)S(1)}, u32[]{:S(2)}, u32[]{:S(2)}) collective-permute-start(bf16[1024,128]{1,0:T(8,128)(2,1)S(1)} %constant_dynamic-update-slice_fusion.2), channel_id=1, source_target_pairs={{0,2},{2,0},{4,6},{6,4},{8,10},{10,8},{12,14},{14,12},{16,18},{18,... | collective-permute-start | bytes 786440 | tf_op jit(solution)/shard_map/ppermute | solution.py:354
  31.6 6.5 %collective-permute-start.10 = (bf16[672,128]{1,0:T(8,128)(2,1)S(1)}, bf16[672,128]{1,0:T(8,128)(2,1)S(1)}, u32[]{:S(2)}, u32[]{:S(2)}) collective-permute-start(bf16[672,128]{1,0:T(8,128)(2,1)S(1)} %get-tuple-element.28.mine_ref), channel_id=1, source_target_pairs={{0,1},{1,0},{2,3},{3,2},{4,5},{5,4},{6,7},{7,6},{8,9},{9,8},{10,11... | collective-permute-start | bytes 516104 | tf_op jit(solution)/shard_map/ppermute | solution.py:401

commit v4 on v3

--- a/solution.py
+++ b/solution.py
@@ -42,7 +42,7 @@
 
 
 def pack_kernel(
-    acts_hbm, cot_hbm, logits_hbm, live_hbm, rows_ref, weights_ref, prob_ref,
+    acts_hbm, cot_hbm, logits_hbm, live_hbm, both_ref, prob_ref,
     acts_ref, cot_ref, logits_ref, live_ref, sems,
 ):
     copies = fetch(
@@ -53,17 +53,18 @@
     per = LANES // depth
     blocks = rows // per
     wide = keys // LANES
+    head_blocks = heads * wide
     copies[0].wait()
     unit, _ = standardize(acts_ref[...])
     normed = unit.astype(BF16)
     for b in range(blocks):
-        rows_ref[pl.ds(b * own, own), :] = jnp.concatenate(
+        both_ref[pl.ds((head_blocks + b) * own, own), :] = jnp.concatenate(
             [normed[b * per + k] for k in range(per)], axis=-1
         )
     copies[1].wait()
     cot = cot_ref[...]
     for b in range(blocks):
-        rows_ref[pl.ds((blocks + b) * own, own), :] = jnp.concatenate(
+        both_ref[pl.ds((head_blocks + blocks + b) * own, own), :] = jnp.concatenate(
             [cot[b * per + k] for k in range(per)], axis=-1
         )
     copies[2].wait()
@@ -76,9 +77,8 @@
         prob_ref[h] = prob
         weights = prob.astype(BF16)
         for w in range(wide):
-            weights_ref[pl.ds((h * wide + w) * own, own), :] = weights[
-                :, w * LANES : (w + 1) * LANES
-            ]
+            block = weights[:, w * LANES : (w + 1) * LANES]
+            both_ref[pl.ds((h * wide + w) * own, own), :] = block
 
 
 def prepare_kernel(
@@ -119,14 +119,27 @@
     inv_ref[...] = jnp.broadcast_to(inv, unit.shape)
 
 
+def place(me, first, count, near_ref, near_beside_ref, far_ref, far_beside_ref, out_ref):
+    parts = out_ref.shape[0]
+    cut = pl.ds(first, count)
+    sources = (near_ref, far_ref, near_beside_ref, far_beside_ref)
+    for low in range(4):
+
+        @pl.when(me % 4 == low)
+        def _():
+            for r in range(parts):
+                level = me // 4 ^ r // 4
+                out_ref[r] = sources[low ^ r % 4][level % 2 * 2 + level // 2, cut]
+
+
 def main_kernel(
     heads,
     where_ref,
     prob_ref,
-    near_rows_ref,
-    far_rows_ref,
-    near_weights_ref,
-    far_weights_ref,
+    near_ref,
+    near_late_ref,
+    far_ref,
+    far_late_ref,
     spread_ref,
     keep_row_ref,
     own_grad_ref,
@@ -151,13 +164,9 @@
     wide = keys // LANES
     first = pl.multiple_of(where_ref[0] * own, own)
     half = where_ref[1]
-    for r in range(parts):
-        away = where_ref[0] ^ r
-        side, column, level = away % 2, away // 2 % 2, away // 4
-        spot = level * 2 + column
-        rows_ref[r] = jnp.where(side == 0, near_rows_ref[spot], far_rows_ref[spot])
-        spot = column * (parts // 4) + level
-        weights_ref[r] = jnp.where(side == 0, near_weights_ref[spot], far_weights_ref[spot])
+    sources = (near_ref, near_late_ref, far_ref, far_late_ref)
+    place(where_ref[0], weights_ref.shape[1], 2 * blocks, *sources, rows_ref)
+    place(where_ref[0], 0, weights_ref.shape[1], *sources, weights_ref)
 
     def row_block(start):
         return jnp.concatenate(
@@ -297,7 +306,7 @@
             ].astype(F32)
 
 
-def call(kernel, outs, spaces, scratch=(), limit=16 * 1024 * 1024, cost=None):
+def call(kernel, outs, spaces, scratch=(), limit=16 * 1024 * 1024, cost=0):
     spec = {
         "v": pl.BlockSpec(memory_space=pltpu.VMEM),
         "s": pl.BlockSpec(memory_space=pltpu.SMEM),
@@ -310,7 +319,9 @@
         out_specs=[spec["v"]] * len(outs),
         scratch_shapes=list(scratch),
         compiler_params=pltpu.CompilerParams(vmem_limit_bytes=limit),
-        cost_estimate=cost,
+        cost_estimate=pl.CostEstimate(
+            flops=cost * 1150000000, bytes_accessed=0, transcendentals=0
+        ),
     )
 
 
@@ -332,11 +343,10 @@
     weight_blocks = heads * keys // LANES
     share = keys // 2
     where = jnp.stack([lax.axis_index("res"), lax.axis_index("seq")]).astype(jnp.int32)
-    packed_rows, packed_weights, prob = call(
+    both, prob = call(
         pack_kernel,
         [
-            ((row_blocks * own, LANES), BF16),
-            ((weight_blocks * own, LANES), BF16),
+            (((row_blocks + weight_blocks) * own, LANES), BF16),
             ((heads, own, keys), F32),
         ],
         "hhhh",
@@ -353,9 +363,6 @@
     def swapped(array, bits):
         return lax.ppermute(array, "res", [(i, i ^ bits) for i in range(parts)])
 
-    def line(array):
-        return jnp.concatenate([array] + [swapped(array, 4 * k) for k in range(1, parts // 4)])
-
     spread, keep_row, unit, inv = call(
         functools.partial(prepare_kernel, heads),
         [
@@ -365,14 +372,19 @@
             ((rows, own, depth), F32),
         ],
         "svvvv",
+        cost=1,
     )(alignment_row_mask, alignment_activations, value_matrix, gate_matrix, output_matrix.T)
-    weights_line = line(packed_weights)
-    rows_pair = jnp.concatenate([packed_rows, swapped(packed_rows, 2)])
-    weights_plane = jnp.concatenate([weights_line, swapped(weights_line, 2)])
-    rows_plane = line(rows_pair)
-
-    def split(array, blocks):
-        return array.reshape(parts // 2, blocks, own, LANES)
+    level_2 = swapped(both, 8)
+    level_1 = swapped(both, 4)
+    beside = swapped(both, 2)
+    level_3 = swapped(level_2, 4)
+    beside_2 = swapped(level_2, 2)
+    beside_13 = swapped(jnp.concatenate([level_1, level_3]), 2)
+    early = jnp.concatenate([both, level_2, level_1, level_3])
+    late = jnp.concatenate([beside, beside_2, beside_13])
+
+    def split(array):
+        return array.reshape(-1, row_blocks + weight_blocks, own, LANES)
 
     own_grad, pair_own, send = call(
         functools.partial(main_kernel, heads),
@@ -388,18 +400,19 @@
         ]
         + [pltpu.VMEM((heads, keys, 2 * LANES), BF16)] * 3,
         32 * 1024 * 1024,
+        cost=5,
     )(
         where,
         prob,
-        split(rows_plane, row_blocks),
-        split(swapped(rows_plane, 1), row_blocks),
-        split(weights_plane, weight_blocks),
-        split(swapped(weights_plane, 1), weight_blocks),
+        split(early),
+        split(late),
+        split(swapped(early, 1)),
+        split(swapped(late, 1)),
         spread,
         keep_row,
     )
     got = lax.ppermute(send, "seq", [(0, 1), (1, 0)])
-    (align,) = call(align_kernel, [((rows, own, depth), F32)], "vvvv")(
+    (align,) = call(align_kernel, [((rows, own, depth), F32)], "vvvv", cost=2)(
         spread, unit, inv, own_grad
     )
     pair, value_total, gate_total, output_total = call(

time: 39.7 us -> 36.7 us (0.924)
  starting transfers between devices: 16 us -> 13.4 us
  waiting for transfers between devices: 8.91 us -> 10.4 us
  other arithmetic: 0.94 us -> 0.09 us
  local copies, waits for them, and re-layouts: 1.8 us -> 1.05 us
    ppermute x10 -> x8, starting transfers between devices: 14.3 us -> 11.6 us  [swapped(): return lax.ppermute(array, 'res', [(i, i ^ bits) for i in range(parts)])]
    ppermute x10 -> x8, waiting for transfers between devices: 5.83 us -> 7.34 us  [swapped(): return lax.ppermute(array, 'res', [(i, i ^ bits) for i in range(parts)])]
    concatenate x1, other arithmetic: 0.86 us -> 0.01 us  [local_gathered(): beside_13 = swapped(jnp.concatenate([level_1, level_3]), 2)]
    unnamed x19 -> x17, local copies, waits for them, and re-layouts: 1.74 us -> 1.01 us
  transfers between devices with their start and end apart: 11 -> 9, of which waited for: 4 -> 5; matrix products, arithmetic and copies ran while one was open for 7% -> 3% of each run, Pallas kernels for 7% -> 7%
where the time goes in v4:
time: 36.7 us; the launch traced here: 36.5 us
  starting transfers between devices  13.4 us (37%)
  Pallas kernels  10.6 us (29%)
  waiting for transfers between devices  10.4 us (28%)
  local copies, waits for them, and re-layouts  1.05 us (3%)
  between operations  0.83 us (2%)
    ppermute x8, starting transfers between devices, swapped(): return lax.ppermute(array, 'res', [(i, i ^ bits) for i in range(parts)])  11.6 us
    ppermute x8, waiting for transfers between devices, swapped(): return lax.ppermute(array, 'res', [(i, i ^ bits) for i in range(parts)])  7.34 us
    pallas_call x1, Pallas kernels, local_gathered(): call(functools.partial(main_kernel, heads), [((2, heads // 2 * rows * wid...  4.69 us
    ppermute x1, waiting for transfers between devices, local_gathered(): got = lax.ppermute(send, 'seq', [(0, 1), (1, 0)])  3.05 us
    pallas_call x1, Pallas kernels, local_gathered(): call(pack_kernel, [(((row_blocks + weight_blocks) * own, LANES), BF16), (...  2.02 us
    ppermute x1, starting transfers between devices, local_gathered(): got = lax.ppermute(send, 'seq', [(0, 1), (1, 0)])  1.81 us
    pallas_call x1, Pallas kernels, local_gathered(): call(align_kernel, [((rows, own, depth), F32)], 'vvvv', cost=2)  1.63 us
    pallas_call x1, Pallas kernels, local_gathered(): call(last_kernel, [((heads, own, share), F32)] + [((depth, width), F32)]...  1.27 us
  transfers between devices with their start and end apart: 9, of which 5 were waited for; matrix products, arithmetic and copies ran while one was open for 3% of the time, Pallas kernels for 7%

profile of v4, /device:TPU:0, one launch (start us, length us, event | category | flops | bytes accessed | tf_op | source)
XLA Modules:
  0.0 36.5 jit_solution(7576871465155296299)
XLA Ops:
  0.6 0.0 copy-start.1
  0.6 0.0 copy-start.5
  0.7 0.0 copy-start.2
  0.7 0.0 copy-start.3
  0.7 0.0 copy-start.4
  0.7 2.0 %shard_map.120 = (bf16[384,128]{1,0:T(8,128)(2,1)}, f32[8,16,256]{2,1,0:T(8,128)}) custom-call(bf16[8,16,64]{2,1,0:T(8,128)(2,1)} %acts_hbm.1, bf16[8,16,64]{2,1,0:T(8,128)(2,1)} %cot_hbm.1, bf16[8,16,256]{2,1,0:T(8,128)(2,1)} %logits_hbm.1, s32[1,256]{1,0:T(1,128)} %bitcast.14), custom_call_target="tpu_custom_call" | custom-call | tf_op jit(solution)/shard_map/pallas_call | solution.py:346
  2.7 4.1 %collective-permute-start = (bf16[384,128]{1,0:T(8,128)(2,1)}, bf16[384,128]{1,0:T(8,128)(2,1)S(1)}, u32[]{:S(2)}, u32[]{:S(2)}) collective-permute-start(bf16[384,128]{1,0:T(8,128)(2,1)} %get-tuple-element.22), channel_id=1, source_target_pairs={{0,16},{2,18},{4,20},{6,22},{8,24},{10,26},{12,28},{14,30},{16,0},... | collective-permute-start | bytes 294920 | tf_op jit(solution)/shard_map/ppermute | solution.py:364
  6.8 1.6 %collective-permute-start.1 = (bf16[384,128]{1,0:T(8,128)(2,1)}, bf16[384,128]{1,0:T(8,128)(2,1)S(1)}, u32[]{:S(2)}, u32[]{:S(2)}) collective-permute-start(bf16[384,128]{1,0:T(8,128)(2,1)} %get-tuple-element.22), channel_id=1, source_target_pairs={{0,8},{2,10},{4,12},{6,14},{8,0},{10,2},{12,4},{14,6},{16,24},{18,... | collective-permute-start | bytes 294920 | tf_op jit(solution)/shard_map/ppermute | solution.py:364
  8.4 1.5 %collective-permute-start.3 = (bf16[384,128]{1,0:T(8,128)(2,1)}, bf16[384,128]{1,0:T(8,128)(2,1)S(1)}, u32[]{:S(2)}, u32[]{:S(2)}) collective-permute-start(bf16[384,128]{1,0:T(8,128)(2,1)} %get-tuple-element.22), channel_id=1, source_target_pairs={{0,4},{2,6},{4,0},{6,2},{8,12},{10,14},{12,8},{14,10},{16,20},{18,... | collective-permute-start | bytes 294920 | tf_op jit(solution)/shard_map/ppermute | solution.py:364
  9.9 0.9 %constant_dynamic-update-slice_fusion.3 = bf16[1536,128]{1,0:T(8,128)(2,1)S(1)} fusion(bf16[384,128]{1,0:T(8,128)(2,1)} %get-tuple-element.22), kind=kLoop, calls=%fused_computation.4 | loop fusion | bytes 196608
  10.8 1.0 %collective-permute-done = bf16[384,128]{1,0:T(8,128)(2,1)S(1)} collective-permute-done((bf16[384,128]{1,0:T(8,128)(2,1)}, bf16[384,128]{1,0:T(8,128)(2,1)S(1)}, u32[]{:S(2)}, u32[]{:S(2)}) %collective-permute-start) | collective-permute-done | bytes 98336 | tf_op jit(solution)/shard_map/ppermute | solution.py:364
  11.8 0.9 %collective-permute-start.2 = (bf16[384,128]{1,0:T(8,128)(2,1)S(1)}, bf16[384,128]{1,0:T(8,128)(2,1)S(1)}, u32[]{:S(2)}, u32[]{:S(2)}) collective-permute-start(bf16[384,128]{1,0:T(8,128)(2,1)S(1)} %collective-permute-done), channel_id=1, source_target_pairs={{0,8},{2,10},{4,12},{6,14},{8,0},{10,2},{12,4},{14,6},{16,24},{18,... | collective-permute-start | bytes 294920 | tf_op jit(solution)/shard_map/ppermute | solution.py:364
  12.8 1.5 %collective-permute-start.4 = (bf16[384,128]{1,0:T(8,128)(2,1)S(1)}, bf16[384,128]{1,0:T(8,128)(2,1)S(1)}, u32[]{:S(2)}, u32[]{:S(2)}) collective-permute-start(bf16[384,128]{1,0:T(8,128)(2,1)S(1)} %collective-permute-done), channel_id=1, source_target_pairs={{0,4},{2,6},{4,0},{6,2},{8,12},{10,14},{12,8},{14,10},{16,20},{18,... | collective-permute-start | bytes 294920 | tf_op jit(solution)/shard_map/ppermute | solution.py:364
  14.3 0.0 collective-permute-done.3
  14.3 0.0 collective-permute-done.1
  14.3 2.1 %collective-permute-done.2 = bf16[384,128]{1,0:T(8,128)(2,1)S(1)} collective-permute-done((bf16[384,128]{1,0:T(8,128)(2,1)S(1)}, bf16[384,128]{1,0:T(8,128)(2,1)S(1)}, u32[]{:S(2)}, u32[]{:S(2)}) %collective-permute-start.2) | collective-permute-done | bytes 98336 | tf_op jit(solution)/shard_map/ppermute | solution.py:364
  16.4 1.8 %collective-permute-start.5 = (bf16[768,128]{1,0:T(8,128)(2,1)S(1)}, bf16[768,128]{1,0:T(8,128)(2,1)S(1)}, u32[]{:S(2)}, u32[]{:S(2)}) collective-permute-start(bf16[768,128]{1,0:T(8,128)(2,1)S(1)} %pad_maximum_fusion), channel_id=1, source_target_pairs={{0,4},{2,6},{4,0},{6,2},{8,12},{10,14},{12,8},{14,10},{16,20},{18,... | collective-permute-start | bytes 589832 | tf_op jit(solution)/shard_map/ppermute | solution.py:364
  18.3 0.1 collective-permute-start.6
  18.4 0.0 collective-permute-done.4
  18.4 3.8 %collective-permute-done.5 = bf16[768,128]{1,0:T(8,128)(2,1)S(1)} collective-permute-done((bf16[768,128]{1,0:T(8,128)(2,1)S(1)}, bf16[768,128]{1,0:T(8,128)(2,1)S(1)}, u32[]{:S(2)}, u32[]{:S(2)}) %collective-permute-start.5) | collective-permute-done | bytes 196640 | tf_op jit(solution)/shard_map/ppermute | solution.py:364
  22.2 0.1 collective-permute-start.7
  22.3 0.0 copy-done.1
  22.3 0.0 copy-done.5
  22.4 1.0 %shard_map.119 = (bf16[3,4,256,256]{3,2,1,0:T(8,128)(2,1)S(1)}, f32[1,256]{1,0:T(1,128)S(1)}, f32[8,16,64]{2,1,0:T(8,128)S(1)}, f32[8,16,64]{2,1,0:T(8,128)S(1)}) custom-call(s32[8]{0:T(128)S(1)} %copy-done.5, bf16[8,16,64]{2,1,0:T(8,128)(2,1)S(1)} %copy-done.1, bf16[64,256]{1,0:T(8,128)(2,1)S(1)} %copy-done.2, bf16[64,256]{1,0:T(8,128)(2,1)S(1)} %copy-done.3, ...), custom_call_target="tpu_custom_call" | custom-call | flops 1150000000 | tf_op jit(solution)/shard_map/pallas_call | solution.py:366
  23.4 0.1 pad_add_fusion.where_ref
  23.5 0.0 collective-permute-done.6
  23.5 0.5 %collective-permute-done.7 = bf16[1536,128]{1,0:T(8,128)(2,1)S(1)} collective-permute-done((bf16[1536,128]{1,0:T(8,128)(2,1)S(1)}, bf16[1536,128]{1,0:T(8,128)(2,1)S(1)}, u32[]{:S(2)}, u32[]{:S(2)}) %collective-permute-start.7) | collective-permute-done | bytes 393248 | tf_op jit(solution)/shard_map/ppermute | solution.py:364
  24.0 4.7 %shard_map.121 = (bf16[2,8,16,256]{3,2,1,0:T(8,128)(2,1)S(1)}, f32[9,16,128]{2,1,0:T(8,128)S(1)}, bf16[672,128]{1,0:T(8,128)(2,1)S(1)}) custom-call(s32[2]{0:T(128)S(1)} %pad_add_fusion.where_ref, f32[8,16,256]{2,1,0:T(8,128)S(1)} %copy-done, bf16[4,24,16,128]{3,2,1,0:T(8,128)(2,1)S(1)} %bitcast.10, bf16[4,24,16,128]{3,2,1,0:T(8,128)(2,1)S(1)} %bitcast.9, ...), custom_call_target="tpu_custom_call" | custom-call | flops 5750000128 | tf_op jit(solution)/shard_map/pallas_call | solution.py:389
  28.7 1.8 %collective-permute-start.8 = (bf16[672,128]{1,0:T(8,128)(2,1)S(1)}, bf16[672,128]{1,0:T(8,128)(2,1)S(1)}, u32[]{:S(2)}, u32[]{:S(2)}) collective-permute-start(bf16[672,128]{1,0:T(8,128)(2,1)S(1)} %get-tuple-element.26.mine_ref), channel_id=1, source_target_pairs={{0,1},{1,0},{2,3},{3,2},{4,5},{5,4},{6,7},{7,6},{8,9},{9,8},{10,11... | collective-permute-start | bytes 516104 | tf_op jit(solution)/shard_map/ppermute | solution.py:414
  30.5 1.6 %shard_map.122 = f32[8,16,64]{2,1,0:T(8,128)} custom-call(bf16[3,4,256,256]{3,2,1,0:T(8,128)(2,1)S(1)} %get-tuple-element.18.spread_ref, f32[8,16,64]{2,1,0:T(8,128)S(1)} %get-tuple-element.19.unit_ref, f32[8,16,64]{2,1,0:T(8,128)S(1)} %get-tuple-element.20.inv_ref, bf16[2,8,16,256]{3,2,1,0:T(8,128)(2,1)S(1)} %get-tuple-element.24.own_grad_ref), custom_call_target="tpu_custom_call" | custom-call | flops 2300000000 | tf_op jit(solution)/shard_map/pallas_call | solution.py:415
  32.1 3.0 %collective-permute-done.8.got_ref = bf16[672,128]{1,0:T(8,128)(2,1)S(1)} collective-permute-done((bf16[672,128]{1,0:T(8,128)(2,1)S(1)}, bf16[672,128]{1,0:T(8,128)(2,1)S(1)}, u32[]{:S(2)}, u32[]{:S(2)}) %collective-permute-start.8) | collective-permute-done | bytes 172064 | tf_op jit(solution)/shard_map/ppermute | solution.py:414
  35.2 1.3 %shard_map.123 = (f32[8,16,128]{2,1,0:T(8,128)}, f32[64,256]{1,0:T(8,128)}, f32[64,256]{1,0:T(8,128)}, f32[64,256]{1,0:T(8,128)}) custom-call(s32[2]{0:T(128)S(1)} %pad_add_fusion.where_ref, f32[8,16,256]{2,1,0:T(8,128)S(1)} %copy-done, f32[9,16,128]{2,1,0:T(8,128)S(1)} %get-tuple-element.25.own_ref, bf16[672,128]{1,0:T(8,128)(2,1)S(1)} %get-tuple-element.26.mine_ref, ...), custom_call_target="tpu_custom_call" | custom-call | tf_op jit(solution)/shard_map/pallas_call | solution.py:418
  (12 shorter events, 0.1 us)
Async XLA Ops:
  0.6 21.7 %copy-start.1 = (bf16[8,16,64]{2,1,0:T(8,128)(2,1)S(1)}, bf16[8,16,64]{2,1,0:T(8,128)(2,1)}, u32[]{:S(2)}) copy-start(bf16[8,16,64]{2,1,0:T(8,128)(2,1)} %acts_hbm.1) | copy-start | bytes 49156
  0.6 21.7 %copy-start.5 = (s32[8]{0:T(128)S(1)}, s32[8]{0:T(128)}, u32[]{:S(2)}) copy-start(s32[8]{0:T(128)} %keep_ref.1) | copy-start | bytes 100
  0.7 21.7 %copy-start.2 = (bf16[64,256]{1,0:T(8,128)(2,1)S(1)}, bf16[64,256]{1,0:T(8,128)(2,1)}, u32[]{:S(2)}) copy-start(bf16[64,256]{1,0:T(8,128)(2,1)} %value_ref.1) | copy-start | bytes 98308
  0.7 21.7 %copy-start.3 = (bf16[64,256]{1,0:T(8,128)(2,1)S(1)}, bf16[64,256]{1,0:T(8,128)(2,1)}, u32[]{:S(2)}) copy-start(bf16[64,256]{1,0:T(8,128)(2,1)} %gate_ref.1) | copy-start | bytes 98308
  0.7 21.7 %copy-start.4 = (bf16[256,64]{0,1:T(8,128)(2,1)S(1)}, bf16[256,64]{0,1:T(8,128)(2,1)}, u32[]{:S(2)}) copy-start(bf16[256,64]{0,1:T(8,128)(2,1)} %param.14) | copy-start | bytes 98308
  2.7 9.1 %collective-permute-start = (bf16[384,128]{1,0:T(8,128)(2,1)}, bf16[384,128]{1,0:T(8,128)(2,1)S(1)}, u32[]{:S(2)}, u32[]{:S(2)}) collective-permute-start(bf16[384,128]{1,0:T(8,128)(2,1)} %get-tuple-element.22), channel_id=1, source_target_pairs={{0,16},{2,18},{4,20},{6,22},{8,24},{10,26},{12,28},{14,30},{16,0},... | collective-permute-start | bytes 294920 | tf_op jit(solution)/shard_map/ppermute | solution.py:364
  6.8 7.5 %collective-permute-start.1 = (bf16[384,128]{1,0:T(8,128)(2,1)}, bf16[384,128]{1,0:T(8,128)(2,1)S(1)}, u32[]{:S(2)}, u32[]{:S(2)}) collective-permute-start(bf16[384,128]{1,0:T(8,128)(2,1)} %get-tuple-element.22), channel_id=1, source_target_pairs={{0,8},{2,10},{4,12},{6,14},{8,0},{10,2},{12,4},{14,6},{16,24},{18,... | collective-permute-start | bytes 294920 | tf_op jit(solution)/shard_map/ppermute | solution.py:364
  8.4 5.9 %collective-permute-start.3 = (bf16[384,128]{1,0:T(8,128)(2,1)}, bf16[384,128]{1,0:T(8,128)(2,1)S(1)}, u32[]{:S(2)}, u32[]{:S(2)}) collective-permute-start(bf16[384,128]{1,0:T(8,128)(2,1)} %get-tuple-element.22), channel_id=1, source_target_pairs={{0,4},{2,6},{4,0},{6,2},{8,12},{10,14},{12,8},{14,10},{16,20},{18,... | collective-permute-start | bytes 294920 | tf_op jit(solution)/shard_map/ppermute | solution.py:364
  11.8 4.6 %collective-permute-start.2 = (bf16[384,128]{1,0:T(8,128)(2,1)S(1)}, bf16[384,128]{1,0:T(8,128)(2,1)S(1)}, u32[]{:S(2)}, u32[]{:S(2)}) collective-permute-start(bf16[384,128]{1,0:T(8,128)(2,1)S(1)} %collective-permute-done), channel_id=1, source_target_pairs={{0,8},{2,10},{4,12},{6,14},{8,0},{10,2},{12,4},{14,6},{16,24},{18,... | collective-permute-start | bytes 294920 | tf_op jit(solution)/shard_map/ppermute | solution.py:364
  12.8 5.6 %collective-permute-start.4 = (bf16[384,128]{1,0:T(8,128)(2,1)S(1)}, bf16[384,128]{1,0:T(8,128)(2,1)S(1)}, u32[]{:S(2)}, u32[]{:S(2)}) collective-permute-start(bf16[384,128]{1,0:T(8,128)(2,1)S(1)} %collective-permute-done), channel_id=1, source_target_pairs={{0,4},{2,6},{4,0},{6,2},{8,12},{10,14},{12,8},{14,10},{16,20},{18,... | collective-permute-start | bytes 294920 | tf_op jit(solution)/shard_map/ppermute | solution.py:364
  16.4 5.7 %collective-permute-start.5 = (bf16[768,128]{1,0:T(8,128)(2,1)S(1)}, bf16[768,128]{1,0:T(8,128)(2,1)S(1)}, u32[]{:S(2)}, u32[]{:S(2)}) collective-permute-start(bf16[768,128]{1,0:T(8,128)(2,1)S(1)} %pad_maximum_fusion), channel_id=1, source_target_pairs={{0,4},{2,6},{4,0},{6,2},{8,12},{10,14},{12,8},{14,10},{16,20},{18,... | collective-permute-start | bytes 589832 | tf_op jit(solution)/shard_map/ppermute | solution.py:364
  18.3 5.2 %collective-permute-start.6 = (bf16[1536,128]{1,0:T(8,128)(2,1)S(1)}, bf16[1536,128]{1,0:T(8,128)(2,1)S(1)}, u32[]{:S(2)}, u32[]{:S(2)}) collective-permute-start(bf16[1536,128]{1,0:T(8,128)(2,1)S(1)} %constant_dynamic-update-slice_fusion), channel_id=1, source_target_pairs={{0,2},{2,0},{4,6},{6,4},{8,10},{10,8},{12,14},{14,12},{16,18},{18,... | collective-permute-start | bytes 1179656 | tf_op jit(solution)/shard_map/ppermute | solution.py:364
  22.2 1.8 %collective-permute-start.7 = (bf16[1536,128]{1,0:T(8,128)(2,1)S(1)}, bf16[1536,128]{1,0:T(8,128)(2,1)S(1)}, u32[]{:S(2)}, u32[]{:S(2)}) collective-permute-start(bf16[1536,128]{1,0:T(8,128)(2,1)S(1)} %constant_dynamic-update-slice_fusion.4), channel_id=1, source_target_pairs={{0,2},{2,0},{4,6},{6,4},{8,10},{10,8},{12,14},{14,12},{16,18},{18,... | collective-permute-start | bytes 1179656 | tf_op jit(solution)/shard_map/ppermute | solution.py:364
  22.4 1.7 %copy-start = (f32[8,16,256]{2,1,0:T(8,128)S(1)}, f32[8,16,256]{2,1,0:T(8,128)}, u32[]{:S(2)}) copy-start(f32[8,16,256]{2,1,0:T(8,128)} %get-tuple-element.21.prob_ref) | copy-start | bytes 393220
  28.7 6.5 %collective-permute-start.8 = (bf16[672,128]{1,0:T(8,128)(2,1)S(1)}, bf16[672,128]{1,0:T(8,128)(2,1)S(1)}, u32[]{:S(2)}, u32[]{:S(2)}) collective-permute-start(bf16[672,128]{1,0:T(8,128)(2,1)S(1)} %get-tuple-element.26.mine_ref), channel_id=1, source_target_pairs={{0,1},{1,0},{2,3},{3,2},{4,5},{5,4},{6,7},{7,6},{8,9},{9,8},{10,11... | collective-permute-start | bytes 516104 | tf_op jit(solution)/shard_map/ppermute | solution.py:414

commit v5 on v4

--- a/solution.py
+++ b/solution.py
@@ -175,8 +175,8 @@
 
     x = [row_block(g * span) for g in range(groups)]
     y = [row_block(blocks + g * span) for g in range(groups)]
-    x_t = [a.T for a in x]
-    y_t = [a.T for a in y]
+    x_t = jnp.concatenate([a.T for a in x], axis=1)
+    y_t = jnp.concatenate([a.T for a in y], axis=1)
 
     lane = lax.broadcasted_iota(jnp.int32, (1, LANES), 1)
     slot = lane // dim
@@ -221,7 +221,7 @@
             )
             vals = jnp.concatenate([v[:, cut] for v in values], axis=1)
             attended = dot(weights, vals)
-            gate = jax.nn.sigmoid(jnp.concatenate([v[:, cut] for v in gates], axis=1))
+            gate = 0.5 + 0.5 * jnp.tanh(0.5 * jnp.concatenate([v[:, cut] for v in gates], axis=1))
             mixed = jnp.concatenate([v[:, cut] for v in mixes], axis=1)
             kept = gate * keep_row
             grad_att = mixed * kept
@@ -236,7 +236,7 @@
             low, high = pair[:, : keys // 2], pair[:, keys // 2 :]
             pair_own_ref[h] = jnp.where(half == 0, low, high)
             put_pair(h, jnp.where(half == 0, high, low))
-        totals = [None, None, None]
+        parts_of = [[], [], []]
         for g in range(groups):
             cut = slice(g * LANES, (g + 1) * LANES)
             mo = jnp.concatenate([a[:, cut] for a in mixed_out], axis=1)
@@ -246,9 +246,12 @@
             val_grad_ref[p * groups + g] = vg
             own_grad_ref[0, p * groups + g] = val_grad_ref[p * groups + g, pl.ds(first, own), :]
             own_grad_ref[1, p * groups + g] = gate_grad_ref[p * groups + g, pl.ds(first, own), :]
-            for t, (left, right) in enumerate(((x_t, vg), (x_t, gg), (y_t, mo))):
-                term = dot(left[g], right)
-                totals[t] = term if totals[t] is None else totals[t] + term
+            for t, part in enumerate((vg, gg, mo)):
+                parts_of[t].append(part)
+        totals = [
+            dot(left, jnp.concatenate(parts_of[t], axis=0))
+            for t, left in enumerate((x_t, x_t, y_t))
+        ]
         for t in range(3):
             folded[t].extend(fold(totals[t]))
 
@@ -379,9 +382,10 @@
     beside = swapped(both, 2)
     level_3 = swapped(level_2, 4)
     beside_2 = swapped(level_2, 2)
-    beside_13 = swapped(jnp.concatenate([level_1, level_3]), 2)
+    beside_1 = swapped(level_1, 2)
+    beside_3 = swapped(level_3, 2)
     early = jnp.concatenate([both, level_2, level_1, level_3])
-    late = jnp.concatenate([beside, beside_2, beside_13])
+    late = jnp.concatenate([beside, beside_2, beside_1, beside_3])
 
     def split(array):
         return array.reshape(-1, row_blocks + weight_blocks, own, LANES)

time: 36.7 us -> 36.1 us (0.984)
  waiting for transfers between devices: 10.4 us -> 9.43 us
  starting transfers between devices: 13.4 us -> 14 us
    ppermute x8 -> x9, waiting for transfers between devices: 7.34 us -> 6.36 us  [swapped(): return lax.ppermute(array, 'res', [(i, i ^ bits) for i in range(parts)])]
    ppermute x8 -> x9, starting transfers between devices: 11.6 us -> 12.2 us  [swapped(): return lax.ppermute(array, 'res', [(i, i ^ bits) for i in range(parts)])]
    unnamed x17 -> x18, local copies, waits for them, and re-layouts: 1.01 us -> 1.02 us
  transfers between devices with their start and end apart: 9 -> 10, of which waited for: 5 -> 6; matrix products, arithmetic and copies ran while one was open for 3% -> 3% of each run, Pallas kernels for 7% -> 7%
where the time goes in v5:
time: 36.1 us; the launch traced here: 35.9 us
  starting transfers between devices  14 us (39%)
  Pallas kernels  10.5 us (29%)
  waiting for transfers between devices  9.43 us (26%)
  local copies, waits for them, and re-layouts  1.05 us (3%)
  between operations  0.82 us (2%)
    ppermute x9, starting transfers between devices, swapped(): return lax.ppermute(array, 'res', [(i, i ^ bits) for i in range(parts)])  12.2 us
    ppermute x9, waiting for transfers between devices, swapped(): return lax.ppermute(array, 'res', [(i, i ^ bits) for i in range(parts)])  6.36 us
    pallas_call x1, Pallas kernels, local_gathered(): call(functools.partial(main_kernel, heads), [((2, heads // 2 * rows * wid...  4.56 us
    ppermute x1, waiting for transfers between devices, local_gathered(): got = lax.ppermute(send, 'seq', [(0, 1), (1, 0)])  3.06 us
    pallas_call x1, Pallas kernels, local_gathered(): call(pack_kernel, [(((row_blocks + weight_blocks) * own, LANES), BF16), (...  2 us
    ppermute x1, starting transfers between devices, local_gathered(): got = lax.ppermute(send, 'seq', [(0, 1), (1, 0)])  1.8 us
    pallas_call x1, Pallas kernels, local_gathered(): call(align_kernel, [((rows, own, depth), F32)], 'vvvv', cost=2)  1.63 us
    pallas_call x1, Pallas kernels, local_gathered(): call(last_kernel, [((heads, own, share), F32)] + [((depth, width), F32)]...  1.27 us
  transfers between devices with their start and end apart: 10, of which 6 were waited for; matrix products, arithmetic and copies ran while one was open for 3% of the time, Pallas kernels for 7%

profile of v5, /device:TPU:0, one launch (start us, length us, event | category | flops | bytes accessed | tf_op | source)
XLA Modules:
  0.0 35.9 jit_solution(12290885481284035859)
XLA Ops:
  0.6 0.0 copy-start.1
  0.6 0.0 copy-start.5
  0.7 0.0 copy-start.2
  0.7 0.0 copy-start.3
  0.7 0.0 copy-start.4
  0.7 2.0 %shard_map.120 = (bf16[384,128]{1,0:T(8,128)(2,1)}, f32[8,16,256]{2,1,0:T(8,128)}) custom-call(bf16[8,16,64]{2,1,0:T(8,128)(2,1)} %acts_hbm.1, bf16[8,16,64]{2,1,0:T(8,128)(2,1)} %cot_hbm.1, bf16[8,16,256]{2,1,0:T(8,128)(2,1)} %logits_hbm.1, s32[1,256]{1,0:T(1,128)} %bitcast.14), custom_call_target="tpu_custom_call" | custom-call | tf_op jit(solution)/shard_map/pallas_call | solution.py:349
  2.7 4.1 %collective-permute-start = (bf16[384,128]{1,0:T(8,128)(2,1)}, bf16[384,128]{1,0:T(8,128)(2,1)S(1)}, u32[]{:S(2)}, u32[]{:S(2)}) collective-permute-start(bf16[384,128]{1,0:T(8,128)(2,1)} %get-tuple-element.22), channel_id=1, source_target_pairs={{0,16},{2,18},{4,20},{6,22},{8,24},{10,26},{12,28},{14,30},{16,0},... | collective-permute-start | bytes 294920 | tf_op jit(solution)/shard_map/ppermute | solution.py:367
  6.8 1.6 %collective-permute-start.1 = (bf16[384,128]{1,0:T(8,128)(2,1)}, bf16[384,128]{1,0:T(8,128)(2,1)S(1)}, u32[]{:S(2)}, u32[]{:S(2)}) collective-permute-start(bf16[384,128]{1,0:T(8,128)(2,1)} %get-tuple-element.22), channel_id=1, source_target_pairs={{0,8},{2,10},{4,12},{6,14},{8,0},{10,2},{12,4},{14,6},{16,24},{18,... | collective-permute-start | bytes 294920 | tf_op jit(solution)/shard_map/ppermute | solution.py:367
  8.4 1.5 %collective-permute-start.3 = (bf16[384,128]{1,0:T(8,128)(2,1)}, bf16[384,128]{1,0:T(8,128)(2,1)S(1)}, u32[]{:S(2)}, u32[]{:S(2)}) collective-permute-start(bf16[384,128]{1,0:T(8,128)(2,1)} %get-tuple-element.22), channel_id=1, source_target_pairs={{0,4},{2,6},{4,0},{6,2},{8,12},{10,14},{12,8},{14,10},{16,20},{18,... | collective-permute-start | bytes 294920 | tf_op jit(solution)/shard_map/ppermute | solution.py:367
  9.9 0.9 %constant_dynamic-update-slice_fusion.3 = bf16[1536,128]{1,0:T(8,128)(2,1)S(1)} fusion(bf16[384,128]{1,0:T(8,128)(2,1)} %get-tuple-element.22), kind=kLoop, calls=%fused_computation.3 | loop fusion | bytes 196608
  10.8 1.0 %collective-permute-done = bf16[384,128]{1,0:T(8,128)(2,1)S(1)} collective-permute-done((bf16[384,128]{1,0:T(8,128)(2,1)}, bf16[384,128]{1,0:T(8,128)(2,1)S(1)}, u32[]{:S(2)}, u32[]{:S(2)}) %collective-permute-start) | collective-permute-done | bytes 98336 | tf_op jit(solution)/shard_map/ppermute | solution.py:367
  11.8 0.9 %collective-permute-start.2 = (bf16[384,128]{1,0:T(8,128)(2,1)S(1)}, bf16[384,128]{1,0:T(8,128)(2,1)S(1)}, u32[]{:S(2)}, u32[]{:S(2)}) collective-permute-start(bf16[384,128]{1,0:T(8,128)(2,1)S(1)} %collective-permute-done), channel_id=1, source_target_pairs={{0,8},{2,10},{4,12},{6,14},{8,0},{10,2},{12,4},{14,6},{16,24},{18,... | collective-permute-start | bytes 294920 | tf_op jit(solution)/shard_map/ppermute | solution.py:367
  12.7 1.5 %collective-permute-start.4 = (bf16[384,128]{1,0:T(8,128)(2,1)S(1)}, bf16[384,128]{1,0:T(8,128)(2,1)S(1)}, u32[]{:S(2)}, u32[]{:S(2)}) collective-permute-start(bf16[384,128]{1,0:T(8,128)(2,1)S(1)} %collective-permute-done), channel_id=1, source_target_pairs={{0,4},{2,6},{4,0},{6,2},{8,12},{10,14},{12,8},{14,10},{16,20},{18,... | collective-permute-start | bytes 294920 | tf_op jit(solution)/shard_map/ppermute | solution.py:367
  14.3 0.0 collective-permute-done.1
  14.3 0.6 %collective-permute-start.5 = (bf16[384,128]{1,0:T(8,128)(2,1)S(1)}, bf16[384,128]{1,0:T(8,128)(2,1)S(1)}, u32[]{:S(2)}, u32[]{:S(2)}) collective-permute-start(bf16[384,128]{1,0:T(8,128)(2,1)S(1)} %collective-permute-done.1), channel_id=1, source_target_pairs={{0,4},{2,6},{4,0},{6,2},{8,12},{10,14},{12,8},{14,10},{16,20},{18,... | collective-permute-start | bytes 294920 | tf_op jit(solution)/shard_map/ppermute | solution.py:367
  14.9 0.0 collective-permute-done.3
  14.9 1.5 %collective-permute-done.2 = bf16[384,128]{1,0:T(8,128)(2,1)S(1)} collective-permute-done((bf16[384,128]{1,0:T(8,128)(2,1)S(1)}, bf16[384,128]{1,0:T(8,128)(2,1)S(1)}, u32[]{:S(2)}, u32[]{:S(2)}) %collective-permute-start.2) | collective-permute-done | bytes 98336 | tf_op jit(solution)/shard_map/ppermute | solution.py:367
  16.4 0.1 collective-permute-start.7
  16.5 1.8 %collective-permute-start.6 = (bf16[384,128]{1,0:T(8,128)(2,1)S(1)}, bf16[384,128]{1,0:T(8,128)(2,1)S(1)}, u32[]{:S(2)}, u32[]{:S(2)}) collective-permute-start(bf16[384,128]{1,0:T(8,128)(2,1)S(1)} %collective-permute-done.2), channel_id=1, source_target_pairs={{0,4},{2,6},{4,0},{6,2},{8,12},{10,14},{12,8},{14,10},{16,20},{18,... | collective-permute-start | bytes 294920 | tf_op jit(solution)/shard_map/ppermute | solution.py:367
  18.4 0.0 collective-permute-done.4
  18.4 1.1 %collective-permute-done.5 = bf16[384,128]{1,0:T(8,128)(2,1)S(1)} collective-permute-done((bf16[384,128]{1,0:T(8,128)(2,1)S(1)}, bf16[384,128]{1,0:T(8,128)(2,1)S(1)}, u32[]{:S(2)}, u32[]{:S(2)}) %collective-permute-start.5) | collective-permute-done | bytes 98336 | tf_op jit(solution)/shard_map/ppermute | solution.py:367
  19.5 2.3 %collective-permute-done.6 = bf16[384,128]{1,0:T(8,128)(2,1)S(1)} collective-permute-done((bf16[384,128]{1,0:T(8,128)(2,1)S(1)}, bf16[384,128]{1,0:T(8,128)(2,1)S(1)}, u32[]{:S(2)}, u32[]{:S(2)}) %collective-permute-start.6) | collective-permute-done | bytes 98336 | tf_op jit(solution)/shard_map/ppermute | solution.py:367
  21.8 0.1 collective-permute-start.8
  21.9 1.0 %shard_map.119 = (bf16[3,4,256,256]{3,2,1,0:T(8,128)(2,1)S(1)}, f32[1,256]{1,0:T(1,128)S(1)}, f32[8,16,64]{2,1,0:T(8,128)S(1)}, f32[8,16,64]{2,1,0:T(8,128)S(1)}) custom-call(s32[8]{0:T(128)S(1)} %copy-done.5, bf16[8,16,64]{2,1,0:T(8,128)(2,1)S(1)} %copy-done.1, bf16[64,256]{1,0:T(8,128)(2,1)S(1)} %copy-done.2, bf16[64,256]{1,0:T(8,128)(2,1)S(1)} %copy-done.3, ...), custom_call_target="tpu_custom_call" | custom-call | flops 1150000000 | tf_op jit(solution)/shard_map/pallas_call | solution.py:369
  23.0 0.1 pad_add_fusion.where_ref
  23.0 0.0 collective-permute-done.7
  23.0 0.5 %collective-permute-done.8 = bf16[1536,128]{1,0:T(8,128)(2,1)S(1)} collective-permute-done((bf16[1536,128]{1,0:T(8,128)(2,1)S(1)}, bf16[1536,128]{1,0:T(8,128)(2,1)S(1)}, u32[]{:S(2)}, u32[]{:S(2)}) %collective-permute-start.8) | collective-permute-done | bytes 393248 | tf_op jit(solution)/shard_map/ppermute | solution.py:367
  23.6 4.6 %shard_map.121 = (bf16[2,8,16,256]{3,2,1,0:T(8,128)(2,1)S(1)}, f32[9,16,128]{2,1,0:T(8,128)S(1)}, bf16[672,128]{1,0:T(8,128)(2,1)S(1)}) custom-call(s32[2]{0:T(128)S(1)} %pad_add_fusion.where_ref, f32[8,16,256]{2,1,0:T(8,128)S(1)} %copy-done, bf16[4,24,16,128]{3,2,1,0:T(8,128)(2,1)S(1)} %bitcast.10, bf16[4,24,16,128]{3,2,1,0:T(8,128)(2,1)S(1)} %bitcast.9, ...), custom_call_target="tpu_custom_call" | custom-call | flops 5750000128 | tf_op jit(solution)/shard_map/pallas_call | solution.py:393
  28.1 1.8 %collective-permute-start.9 = (bf16[672,128]{1,0:T(8,128)(2,1)S(1)}, bf16[672,128]{1,0:T(8,128)(2,1)S(1)}, u32[]{:S(2)}, u32[]{:S(2)}) collective-permute-start(bf16[672,128]{1,0:T(8,128)(2,1)S(1)} %get-tuple-element.26.mine_ref), channel_id=1, source_target_pairs={{0,1},{1,0},{2,3},{3,2},{4,5},{5,4},{6,7},{7,6},{8,9},{9,8},{10,11... | collective-permute-start | bytes 516104 | tf_op jit(solution)/shard_map/ppermute | solution.py:418
  29.9 1.6 %shard_map.122 = f32[8,16,64]{2,1,0:T(8,128)} custom-call(bf16[3,4,256,256]{3,2,1,0:T(8,128)(2,1)S(1)} %get-tuple-element.18.spread_ref, f32[8,16,64]{2,1,0:T(8,128)S(1)} %get-tuple-element.19.unit_ref, f32[8,16,64]{2,1,0:T(8,128)S(1)} %get-tuple-element.20.inv_ref, bf16[2,8,16,256]{3,2,1,0:T(8,128)(2,1)S(1)} %get-tuple-element.24.own_grad_ref), custom_call_target="tpu_custom_call" | custom-call | flops 2300000000 | tf_op jit(solution)/shard_map/pallas_call | solution.py:419
  31.5 3.1 %collective-permute-done.9.got_ref = bf16[672,128]{1,0:T(8,128)(2,1)S(1)} collective-permute-done((bf16[672,128]{1,0:T(8,128)(2,1)S(1)}, bf16[672,128]{1,0:T(8,128)(2,1)S(1)}, u32[]{:S(2)}, u32[]{:S(2)}) %collective-permute-start.9) | collective-permute-done | bytes 172064 | tf_op jit(solution)/shard_map/ppermute | solution.py:418
  34.6 1.3 %shard_map.123 = (f32[8,16,128]{2,1,0:T(8,128)}, f32[64,256]{1,0:T(8,128)}, f32[64,256]{1,0:T(8,128)}, f32[64,256]{1,0:T(8,128)}) custom-call(s32[2]{0:T(128)S(1)} %pad_add_fusion.where_ref, f32[8,16,256]{2,1,0:T(8,128)S(1)} %copy-done, f32[9,16,128]{2,1,0:T(8,128)S(1)} %get-tuple-element.25.own_ref, bf16[672,128]{1,0:T(8,128)(2,1)S(1)} %get-tuple-element.26.mine_ref, ...), custom_call_target="tpu_custom_call" | custom-call | tf_op jit(solution)/shard_map/pallas_call | solution.py:422
  (14 shorter events, 0.1 us)
Async XLA Ops:
  0.6 21.2 %copy-start.1 = (bf16[8,16,64]{2,1,0:T(8,128)(2,1)S(1)}, bf16[8,16,64]{2,1,0:T(8,128)(2,1)}, u32[]{:S(2)}) copy-start(bf16[8,16,64]{2,1,0:T(8,128)(2,1)} %acts_hbm.1) | copy-start | bytes 49156
  0.6 21.2 %copy-start.5 = (s32[8]{0:T(128)S(1)}, s32[8]{0:T(128)}, u32[]{:S(2)}) copy-start(s32[8]{0:T(128)} %keep_ref.1) | copy-start | bytes 100
  0.7 21.2 %copy-start.2 = (bf16[64,256]{1,0:T(8,128)(2,1)S(1)}, bf16[64,256]{1,0:T(8,128)(2,1)}, u32[]{:S(2)}) copy-start(bf16[64,256]{1,0:T(8,128)(2,1)} %value_ref.1) | copy-start | bytes 98308
  0.7 21.2 %copy-start.3 = (bf16[64,256]{1,0:T(8,128)(2,1)S(1)}, bf16[64,256]{1,0:T(8,128)(2,1)}, u32[]{:S(2)}) copy-start(bf16[64,256]{1,0:T(8,128)(2,1)} %gate_ref.1) | copy-start | bytes 98308
  0.7 21.2 %copy-start.4 = (bf16[256,64]{0,1:T(8,128)(2,1)S(1)}, bf16[256,64]{0,1:T(8,128)(2,1)}, u32[]{:S(2)}) copy-start(bf16[256,64]{0,1:T(8,128)(2,1)} %param.14) | copy-start | bytes 98308
  2.7 9.1 %collective-permute-start = (bf16[384,128]{1,0:T(8,128)(2,1)}, bf16[384,128]{1,0:T(8,128)(2,1)S(1)}, u32[]{:S(2)}, u32[]{:S(2)}) collective-permute-start(bf16[384,128]{1,0:T(8,128)(2,1)} %get-tuple-element.22), channel_id=1, source_target_pairs={{0,16},{2,18},{4,20},{6,22},{8,24},{10,26},{12,28},{14,30},{16,0},... | collective-permute-start | bytes 294920 | tf_op jit(solution)/shard_map/ppermute | solution.py:367
  6.8 7.5 %collective-permute-start.1 = (bf16[384,128]{1,0:T(8,128)(2,1)}, bf16[384,128]{1,0:T(8,128)(2,1)S(1)}, u32[]{:S(2)}, u32[]{:S(2)}) collective-permute-start(bf16[384,128]{1,0:T(8,128)(2,1)} %get-tuple-element.22), channel_id=1, source_target_pairs={{0,8},{2,10},{4,12},{6,14},{8,0},{10,2},{12,4},{14,6},{16,24},{18,... | collective-permute-start | bytes 294920 | tf_op jit(solution)/shard_map/ppermute | solution.py:367
  8.4 6.5 %collective-permute-start.3 = (bf16[384,128]{1,0:T(8,128)(2,1)}, bf16[384,128]{1,0:T(8,128)(2,1)S(1)}, u32[]{:S(2)}, u32[]{:S(2)}) collective-permute-start(bf16[384,128]{1,0:T(8,128)(2,1)} %get-tuple-element.22), channel_id=1, source_target_pairs={{0,4},{2,6},{4,0},{6,2},{8,12},{10,14},{12,8},{14,10},{16,20},{18,... | collective-permute-start | bytes 294920 | tf_op jit(solution)/shard_map/ppermute | solution.py:367
  11.8 4.6 %collective-permute-start.2 = (bf16[384,128]{1,0:T(8,128)(2,1)S(1)}, bf16[384,128]{1,0:T(8,128)(2,1)S(1)}, u32[]{:S(2)}, u32[]{:S(2)}) collective-permute-start(bf16[384,128]{1,0:T(8,128)(2,1)S(1)} %collective-permute-done), channel_id=1, source_target_pairs={{0,8},{2,10},{4,12},{6,14},{8,0},{10,2},{12,4},{14,6},{16,24},{18,... | collective-permute-start | bytes 294920 | tf_op jit(solution)/shard_map/ppermute | solution.py:367
  12.7 5.6 %collective-permute-start.4 = (bf16[384,128]{1,0:T(8,128)(2,1)S(1)}, bf16[384,128]{1,0:T(8,128)(2,1)S(1)}, u32[]{:S(2)}, u32[]{:S(2)}) collective-permute-start(bf16[384,128]{1,0:T(8,128)(2,1)S(1)} %collective-permute-done), channel_id=1, source_target_pairs={{0,4},{2,6},{4,0},{6,2},{8,12},{10,14},{12,8},{14,10},{16,20},{18,... | collective-permute-start | bytes 294920 | tf_op jit(solution)/shard_map/ppermute | solution.py:367
  14.3 5.2 %collective-permute-start.5 = (bf16[384,128]{1,0:T(8,128)(2,1)S(1)}, bf16[384,128]{1,0:T(8,128)(2,1)S(1)}, u32[]{:S(2)}, u32[]{:S(2)}) collective-permute-start(bf16[384,128]{1,0:T(8,128)(2,1)S(1)} %collective-permute-done.1), channel_id=1, source_target_pairs={{0,4},{2,6},{4,0},{6,2},{8,12},{10,14},{12,8},{14,10},{16,20},{18,... | collective-permute-start | bytes 294920 | tf_op jit(solution)/shard_map/ppermute | solution.py:367
  16.4 6.6 %collective-permute-start.7 = (bf16[1536,128]{1,0:T(8,128)(2,1)S(1)}, bf16[1536,128]{1,0:T(8,128)(2,1)S(1)}, u32[]{:S(2)}, u32[]{:S(2)}) collective-permute-start(bf16[1536,128]{1,0:T(8,128)(2,1)S(1)} %constant_dynamic-update-slice_fusion), channel_id=1, source_target_pairs={{0,2},{2,0},{4,6},{6,4},{8,10},{10,8},{12,14},{14,12},{16,18},{18,... | collective-permute-start | bytes 1179656 | tf_op jit(solution)/shard_map/ppermute | solution.py:367
  16.5 5.2 %collective-permute-start.6 = (bf16[384,128]{1,0:T(8,128)(2,1)S(1)}, bf16[384,128]{1,0:T(8,128)(2,1)S(1)}, u32[]{:S(2)}, u32[]{:S(2)}) collective-permute-start(bf16[384,128]{1,0:T(8,128)(2,1)S(1)} %collective-permute-done.2), channel_id=1, source_target_pairs={{0,4},{2,6},{4,0},{6,2},{8,12},{10,14},{12,8},{14,10},{16,20},{18,... | collective-permute-start | bytes 294920 | tf_op jit(solution)/shard_map/ppermute | solution.py:367
  21.8 1.8 %collective-permute-start.8 = (bf16[1536,128]{1,0:T(8,128)(2,1)S(1)}, bf16[1536,128]{1,0:T(8,128)(2,1)S(1)}, u32[]{:S(2)}, u32[]{:S(2)}) collective-permute-start(bf16[1536,128]{1,0:T(8,128)(2,1)S(1)} %constant_dynamic-update-slice_fusion.4), channel_id=1, source_target_pairs={{0,2},{2,0},{4,6},{6,4},{8,10},{10,8},{12,14},{14,12},{16,18},{18,... | collective-permute-start | bytes 1179656 | tf_op jit(solution)/shard_map/ppermute | solution.py:367
  21.9 1.7 %copy-start = (f32[8,16,256]{2,1,0:T(8,128)S(1)}, f32[8,16,256]{2,1,0:T(8,128)}, u32[]{:S(2)}) copy-start(f32[8,16,256]{2,1,0:T(8,128)} %get-tuple-element.21.prob_ref) | copy-start | bytes 393220
  28.1 6.5 %collective-permute-start.9 = (bf16[672,128]{1,0:T(8,128)(2,1)S(1)}, bf16[672,128]{1,0:T(8,128)(2,1)S(1)}, u32[]{:S(2)}, u32[]{:S(2)}) collective-permute-start(bf16[672,128]{1,0:T(8,128)(2,1)S(1)} %get-tuple-element.26.mine_ref), channel_id=1, source_target_pairs={{0,1},{1,0},{2,3},{3,2},{4,5},{5,4},{6,7},{7,6},{8,9},{9,8},{10,11... | collective-permute-start | bytes 516104 | tf_op jit(solution)/shard_map/ppermute | solution.py:418
